TPU v7x, 32 devices: a whole 2x2x4 slice. The times are simulated.
32 devices in a mesh: gx: 8 (over z, x), gy: 4 (over y, core).
Axes of the slice: x: 2, y: 2, z: 4, core: 2. Of those that a mesh axis runs over, the one named last changes fastest.
Arguments:
- distribution_values: float32 [19, 16, 32, 128], P(None, 'gx', 'gy'), may hold values from 0.02 to 0.09
- thermal_field: float32 [16, 32, 128], P('gx', 'gy'), may hold values from -0.5 to 0.5
- site_kind_code: int32 [16, 32, 128], P('gx', 'gy'), may hold values from 0 to 2, as said below
- entry_level_matrix: float32 [19, 128], replicated, may hold values from -16 to 16
- entry_level_offset: float32 [128], replicated, may hold values from -3 to 3
- inner_level_matrix: float32 [128, 128], replicated, may hold values from -0.5 to 0.5
- inner_level_offset: float32 [128], replicated, may hold values from -3 to 3
- exit_level_matrix: float32 [128, 19], replicated, may hold values from -0.125 to 0.125
- exit_level_offset: float32 [19], replicated, may hold values from -0.75 to 0.75
- closing_density_adjoint: float32 [19, 16, 32, 128], P(None, 'gx', 'gy'), may hold values from -6 to 6
- closing_thermal_adjoint: float32 [16, 32, 128], P('gx', 'gy'), may hold values from -6 to 6
Outputs:
- adjoint_populations: float32 [19, 16, 32, 128], P(None, 'gx', 'gy')
- adjoint_temperature: float32 [16, 32, 128], P('gx', 'gy')
- grad_first_weight: float32 [19, 128], replicated
- grad_first_bias: float32 [128], replicated
- grad_second_weight: float32 [128, 128], replicated
- grad_second_bias: float32 [128], replicated
- grad_third_weight: float32 [128, 19], replicated
- grad_third_bias: float32 [19], replicated
Inputs may be any that keep to these rules, and one draw needn't show every extreme that they name: `site_kind_code`: 0 marks a fluid cell, 1 a solid cell whose temperature is held, 2 a solid heater cell.
All inputs are finite; a program needn't handle non-finite values.
Results may differ from a plain program's by a relative error of at most 0.0003.
Values sent between devices are 32-bit elements; how exact they have to be, the bound alone decides.
A program may use at most 64 MiB of HBM per device.

v0:
```python
import math

import jax
import jax.numpy as jnp
import numpy as np
from jax import lax
from jax.sharding import PartitionSpec as P

STEPS = 2


VELOCITIES = np.array(
    [
        [0, 0, 0],
        [1, 0, 0],
        [-1, 0, 0],
        [0, 1, 0],
        [0, -1, 0],
        [0, 0, 1],
        [0, 0, -1],
        [1, 1, 0],
        [-1, -1, 0],
        [1, -1, 0],
        [-1, 1, 0],
        [1, 0, 1],
        [-1, 0, -1],
        [1, 0, -1],
        [-1, 0, 1],
        [0, 1, 1],
        [0, -1, -1],
        [0, 1, -1],
        [0, -1, 1],
    ]
)
OPPOSITE = np.array([0, 2, 1, 4, 3, 6, 5, 8, 7, 10, 9, 12, 11, 14, 13, 16, 15, 18, 17])
LATTICE_WEIGHTS = np.array([1.0 / 3.0] + [1.0 / 18.0] * 6 + [1.0 / 36.0] * 12)
BUOYANCY = 0.3 * LATTICE_WEIGHTS * VELOCITIES[:, 2]
PLANE_DIRECTIONS = [(0, 1), (0, -1), (1, 1), (1, -1)]
CONDUCTIVITY = 0.1
HOT_WALL = 0.5
COLD_WALL = -0.5
HEATER = 0.5
PRECISE_MODE = lax.Precision.HIGHEST
CONTRACT = (((0,), (0,)), ((), ()))


def with_halo(block, sides, width):
    for axis, dim in sides:
        count = lax.axis_size(axis)
        forward = [(i, i + 1) for i in range(count - 1)]
        forward.append((count - 1, 0))
        backward = [(target, source) for source, target in forward]
        low = lax.ppermute(
            lax.slice_in_dim(block, block.shape[dim] - width, None, axis=dim), axis, forward
        )
        high = lax.ppermute(lax.slice_in_dim(block, 0, width, axis=dim), axis, backward)
        block = jnp.concatenate([low, block, high], axis=dim)
    return block


def propagation_offset(window, step_z):
    lead = [(0, 0)] * (window.ndim - 1)
    if step_z == 1:
        return jnp.pad(window[..., :-1], lead + [(1, 0)])
    if step_z == -1:
        return jnp.pad(window[..., 1:], lead + [(0, 1)])
    return window


def boundary(cells):
    depths = jnp.arange(cells)
    masks = []
    for i in range(19):
        step_z = int(VELOCITIES[i, 2])
        if step_z == 1:
            masks.append(depths == 0)
        elif step_z == -1:
            masks.append(depths == cells - 1)
        else:
            masks.append(depths < 0)
    return jnp.stack(masks).astype(jnp.float32)[:, None, None, :]


def collide(current_fields, current_thermal, site_kind_code, learned_coefficients):
    (
        entry_level_matrix,
        entry_level_offset,
        inner_level_matrix,
        inner_level_offset,
        exit_level_matrix,
        exit_level_offset,
    ) = learned_coefficients
    flattened = current_fields.reshape(19, -1)
    hidden_one = jnp.tanh(
        lax.dot_general(entry_level_matrix, flattened, CONTRACT, precision=PRECISE_MODE)
        + entry_level_offset[:, None]
    )
    hidden_two = jnp.tanh(
        lax.dot_general(inner_level_matrix, hidden_one, CONTRACT, precision=PRECISE_MODE)
        + inner_level_offset[:, None]
    )
    output = (
        lax.dot_general(exit_level_matrix, hidden_two, CONTRACT, precision=PRECISE_MODE)
        + exit_level_offset[:, None]
    )
    lifting = jnp.asarray(BUOYANCY, jnp.float32).reshape((19,) + (1,) * current_thermal.ndim)
    relaxed = (
        current_fields + output.reshape(current_fields.shape) + lifting * current_thermal[None]
    )
    bounced = current_fields[OPPOSITE]
    return jnp.where(site_kind_code[None] == 0, relaxed, bounced)


def motion_of(current_fields):
    lookup_table = jnp.asarray(VELOCITIES.T, jnp.float32)
    return jnp.tensordot(lookup_table, current_fields, axes=1, precision=PRECISE_MODE)


def depth_pad(heat_rim):
    span_along_x, span_along_y, discarded_outcome = heat_rim.shape
    bottom = jnp.full((span_along_x, span_along_y, 1), HOT_WALL, jnp.float32)
    upper = jnp.full((span_along_x, span_along_y, 1), COLD_WALL, jnp.float32)
    return jnp.concatenate([bottom, heat_rim, upper], axis=2)


def advance_temp(padded, current_thermal, motion, site_kind_code):
    span_along_x, span_along_y, span_along_z = current_thermal.shape
    summed = (1.0 - 6.0 * CONDUCTIVITY) * current_thermal
    for a in range(3):
        for s in (1, -1):
            anchor = [1, 1, 1]
            anchor[a] += s
            nearby = padded[
                anchor[0] : anchor[0] + span_along_x,
                anchor[1] : anchor[1] + span_along_y,
                anchor[2] : anchor[2] + span_along_z,
            ]
            summed = summed + (CONDUCTIVITY - 0.5 * s * motion[a]) * nearby
    return jnp.where(
        site_kind_code == 0, summed, jnp.where(site_kind_code == 1, current_thermal, HEATER)
    )


def stream_pull(planes, orient):
    span_along_x = planes[0].shape[0] - 2
    span_along_y = planes[0].shape[1] - 2
    pulled = []
    for i in range(19):
        step_x = int(VELOCITIES[i, 0]) * orient
        step_y = int(VELOCITIES[i, 1]) * orient
        step_z = int(VELOCITIES[i, 2]) * orient
        window = planes[i][
            1 - step_x : 1 - step_x + span_along_x, 1 - step_y : 1 - step_y + span_along_y, :
        ]
        pulled.append(propagation_offset(window, step_z))
    return jnp.stack(pulled)


def forward_rims(post_collide, current_thermal):
    stacked = jnp.concatenate([post_collide, current_thermal[None]], axis=0)
    padded = with_halo(stacked, (("gx", 1), ("gy", 2)), 1)
    return ([padded[i] for i in range(19)], padded[-1])


def adjoint_rims(current_adjoint, fluxes):
    stacked = jnp.concatenate([current_adjoint, fluxes], axis=0)
    padded = with_halo(stacked, (("gx", 1), ("gy", 2)), 1)
    return ([padded[i] for i in range(19)], padded[-4:])


def per_device(
    distribution_values,
    thermal_field,
    site_kind_code,
    entry_level_matrix,
    entry_level_offset,
    inner_level_matrix,
    inner_level_offset,
    exit_level_matrix,
    exit_level_offset,
    closing_density_adjoint,
    closing_thermal_adjoint,
):
    learned_coefficients = (
        entry_level_matrix,
        entry_level_offset,
        inner_level_matrix,
        inner_level_offset,
        exit_level_matrix,
        exit_level_offset,
    )
    span_along_x, span_along_y, span_along_z = thermal_field.shape
    walls = boundary(span_along_z)
    history = []
    current_fields, current_thermal = (distribution_values, thermal_field)
    for i in range(STEPS):
        post_collide = collide(
            current_fields, current_thermal, site_kind_code, learned_coefficients
        )
        planes, heat_rim = forward_rims(post_collide, current_thermal)
        read = stream_pull(planes, 1) + walls * post_collide[OPPOSITE]
        motion = motion_of(current_fields)
        heated = advance_temp(depth_pad(heat_rim), current_thermal, motion, site_kind_code)
        history.append((current_fields, current_thermal, heat_rim, motion))
        current_fields, current_thermal = (read, heated)
    is_fluid = (site_kind_code == 0).astype(jnp.float32)
    constant_inputs = (site_kind_code == 1).astype(jnp.float32)
    lookup_table = jnp.asarray(VELOCITIES, jnp.float32)
    current_adjoint, thermal_adjoint = (closing_density_adjoint, closing_thermal_adjoint)
    accumulated = None
    for i in reversed(range(STEPS)):
        current_fields, current_thermal, heat_rim, motion = history[i]
        liquid_adjoint = is_fluid * thermal_adjoint
        fluxes = jnp.stack(
            [(CONDUCTIVITY - 0.5 * s * motion[a]) * liquid_adjoint for a, s in PLANE_DIRECTIONS]
        )
        planes, flux_rim = adjoint_rims(current_adjoint, fluxes)
        postcollision_gradient = stream_pull(planes, -1) + (walls * current_adjoint)[OPPOSITE]
        thermal_adjoint_increment = (
            1.0 - 6.0 * CONDUCTIVITY
        ) * liquid_adjoint + constant_inputs * thermal_adjoint
        for j in range(4):
            along, s = PLANE_DIRECTIONS[j]
            anchor = [1, 1]
            anchor[along] -= s
            thermal_adjoint_increment = (
                thermal_adjoint_increment
                + flux_rim[
                    j, anchor[0] : anchor[0] + span_along_x, anchor[1] : anchor[1] + span_along_y, :
                ]
            )
        for s in (1, -1):
            thermal_adjoint_increment = thermal_adjoint_increment + propagation_offset(
                (CONDUCTIVITY - 0.5 * s * motion[2]) * liquid_adjoint, s
            )
        full_rim = depth_pad(heat_rim)
        motion_gradient = []
        for a in range(3):
            summed = jnp.zeros_like(current_thermal)
            for s in (1, -1):
                anchor = [1, 1, 1]
                anchor[a] += s
                nearby = full_rim[
                    anchor[0] : anchor[0] + span_along_x,
                    anchor[1] : anchor[1] + span_along_y,
                    anchor[2] : anchor[2] + span_along_z,
                ]
                summed = summed - 0.5 * s * nearby
            motion_gradient.append(liquid_adjoint * summed)
        discarded_outcome, backpropagation_function = jax.vjp(
            lambda p, h, w: collide(p, h, site_kind_code, w),
            current_fields,
            current_thermal,
            learned_coefficients,
        )
        collision_gradient, relaxation_thermal_adjoint, adjoint_sequence = backpropagation_function(
            postcollision_gradient
        )
        current_adjoint = collision_gradient + jnp.tensordot(
            lookup_table, jnp.stack(motion_gradient), axes=1, precision=PRECISE_MODE
        )
        thermal_adjoint = thermal_adjoint_increment + relaxation_thermal_adjoint
        accumulated = (
            adjoint_sequence
            if accumulated is None
            else jax.tree.map(jnp.add, accumulated, adjoint_sequence)
        )
    finals = lax.psum(
        (
            accumulated[0],
            accumulated[1],
            accumulated[2],
            accumulated[3],
            accumulated[4],
            accumulated[5],
        ),
        ("gx", "gy"),
    )
    factor = 1.0 / math.sqrt(
        span_along_x * lax.axis_size("gx") * span_along_y * lax.axis_size("gy") * span_along_z
    )
    return (
        current_adjoint,
        thermal_adjoint,
        finals[0] * factor,
        finals[1] * factor,
        finals[2] * factor,
        finals[3] * factor,
        finals[4] * factor,
        finals[5] * factor,
    )


def solution(mesh):
    in_specs = (
        P(None, "gx", "gy", None),
        P("gx", "gy", None),
        P("gx", "gy", None),
        P(),
        P(),
        P(),
        P(),
        P(),
        P(),
        P(None, "gx", "gy", None),
        P("gx", "gy", None),
    )
    out_specs = (P(None, "gx", "gy", None), P("gx", "gy", None), P(), P(), P(), P(), P(), P())
    return jax.shard_map(
        per_device, mesh=mesh, in_specs=in_specs, out_specs=out_specs, check_vma=False
    )
```

profile of v0, /device:TPU:0, one launch (start us, length us, event | category | flops | bytes accessed | tf_op | source)
XLA Modules:
  0.0 326.1 jit_solution(10453520149503858511)
XLA Ops:
  8.0 1.5 gather_fusion
  11.4 1.8 fusion.4
  15.1 3.0 collective-permute-start
  18.1 3.1 collective-permute-start.1
  24.4 1.7 collective-permute-start.3
  33.5 4.0 %collective-permute-start.5 = (f32[23,1,8,128]{3,2,1,0:T(8,128)}, f32[23,1,8,128]{3,2,1,0:T(8,128)}, u32[]{:S(2)}, u32[]{:S(2)}) collective-permute-start(f32[23,1,8,128]{3,2,1,0:T(8,128)} %get-tuple-element.91), channel_id=1, source_target_pairs={{4,0},{8,4},{12,8},{16,12},{20,16},{24,20},{28,24},{0,28},{5,1},{9... | collective-permute-start | bytes 282632 | tf_op jit(solution)/shard_map/ppermute | solution.py:56
  38.3 2.1 stack.457
  41.1 2.9 fusion
  45.9 1.7 convolution_add_fusion.4
  47.7 1.7 pad_maximum_fusion.8
  51.7 2.3 gather_fusion.3
  54.0 2.3 gather_fusion.2
  76.9 4.4 %stack.437 = f32[19,2048]{1,0:T(8,128)} concatenate(f32[1,2048]{1,0:T(1,128)} %bitcast.635, f32[1,2048]{1,0:T(1,128)} %bitcast.644, f32[1,2048]{1,0:T(1,128)} %bitcast.643, f32[1,2048]{1,0:T(1,128)} %bitcast.642, f32[1,2048]{1,0:T(1,128)} %bitcast.650, f32[1,2048]{1,0:T(1,128)} %bitcast.648, f32[1,2048]{1,0:T(1,128)} %bitcast.649, f32[1,2048]{1,0:T(1,128)} %bitcast.638, ...), dimensions={0} | concatenate | bytes 311296 | tf_op jit(solution)/shard_map/stack | solution.py:156
  81.3 2.7 fusion.21
  84.1 2.4 fusion.83
  86.5 2.5 fusion.87
  89.0 1.5 fusion.81
  104.3 1.4 multiply_bitcast_fusion.3
  106.8 4.7 %collective-permute-start.9 = (f32[20,1,8,128]{3,2,1,0:T(8,128)S(1)}, f32[20,1,8,128]{3,2,1,0:T(8,128)S(1)}, u32[]{:S(2)}, u32[]{:S(2)}) collective-permute-start(f32[20,1,8,128]{3,2,1,0:T(8,128)S(1)} %get-tuple-element.95), channel_id=1, source_target_pairs={{4,0},{8,4},{12,8},{16,12},{20,16},{24,20},{28,24},{0,28},{5,1},{9... | collective-permute-start | bytes 245768 | tf_op jit(solution)/shard_map/ppermute | solution.py:56
  114.1 1.7 collective-permute-start.11
  115.9 1.6 collective-permute-done.10
  119.4 1.8 scatter_fusion
  121.3 4.8 %collective-permute-start.13 = (f32[23,1,8,128]{3,2,1,0:T(8,128)S(1)}, f32[23,1,8,128]{3,2,1,0:T(8,128)S(1)}, u32[]{:S(2)}, u32[]{:S(2)}) collective-permute-start(f32[23,1,8,128]{3,2,1,0:T(8,128)S(1)} %get-tuple-element.89), channel_id=1, source_target_pairs={{4,0},{8,4},{12,8},{16,12},{20,16},{24,20},{28,24},{0,28},{5,1},{9... | collective-permute-start | bytes 282632 | tf_op jit(solution)/shard_map/ppermute | solution.py:56
  126.5 2.2 collective-permute-done.12
  129.6 1.6 collective-permute-start.15
  147.2 1.7 stack.505
  149.0 1.8 fusion.84
  152.8 1.8 convolution_add_fusion.6
  158.4 40.7 %all-reduce.38 = (f32[19,128]{1,0:T(8,128)S(1)}, f32[128]{0:T(128)S(1)}, f32[128]{0:T(128)S(1)}, f32[128,19]{0,1:T(8,128)S(1)}, f32[19]{0:T(128)S(1)}) all-reduce(f32[19,128]{1,0:T(8,128)S(1)} %fusion.5, f32[128]{0:T(128)S(1)} %add.371, f32[128]{0:T(128)S(1)} %add.373, ...), channel_id=1, replica_groups=mesh['gx'=8,'gy'=4] {'gx','gy'}, use_global_device_ids=true, to_apply=%region_4.5 | all-reduce | flops 5139 | bytes 41112 | tf_op jit(solution)/shard_map/psum | solution.py:268
  204.0 1.8 scatter_fusion.1
  205.7 112.1 %all-reduce.41.cloned.1.call-done = f32[128,128]{1,0:T(8,128)} async-done(((f32[128,128]{1,0:T(8,128)}), f32[128,128]{1,0:T(8,128)}) %all-reduce.41.cloned.1.call-update) | async-done | bytes 65552 | tf_op jit(solution)/shard_map/psum | solution.py:268
  317.8 1.5 broadcast_multiply_fusion.2
  (490 shorter events, 88.0 us)
Async XLA Ops:
  7.2 4.2 %copy-start = (f32[128,128]{1,0:T(8,128)S(1)}, f32[128,128]{1,0:T(8,128)}, u32[]{:S(2)}) copy-start(f32[128,128]{1,0:T(8,128)} %param.31) | copy-start | bytes 196612
  7.2 310.6 %all-reduce.41.cloned.1.call-start = ((), (), s32[]{:S(2)}) async-start(), calls=%async_computation | async-start | bytes 131072 | tf_op jit(solution)/shard_map/psum | solution.py:268
  8.0 18.2 %copy-start.96 = (s32[1024]{0:T(1024)}, s32[1024]{0:T(1024)S(1)}, u32[]{:S(2)}) copy-start(s32[1024]{0:T(1024)S(1)} %pad_clamp_fusion) | copy-start | bytes 12292
  15.1 6.1 %copy-start.98 = (f32[3,19,1,1]{1,0,3,2:T(4,128)S(1)}, f32[3,19,1,1]{1,0,3,2:T(4,128)}, u32[]{:S(2)}) copy-start(f32[3,19,1,1]{1,0,3,2:T(4,128)} %constant.148) | copy-start | bytes 688
  15.1 8.6 %collective-permute-start = (f32[20,1,8,128]{3,2,1,0:T(8,128)S(1)}, f32[20,1,8,128]{3,2,1,0:T(8,128)S(1)}, u32[]{:S(2)}, u32[]{:S(2)}) collective-permute-start(f32[20,1,8,128]{3,2,1,0:T(8,128)S(1)} %get-tuple-element.96), channel_id=1, source_target_pairs={{0,4},{4,8},{8,12},{12,16},{16,20},{20,24},{24,28},{28,0},{1,5},{5... | collective-permute-start | bytes 245768 | tf_op jit(solution)/shard_map/ppermute | solution.py:53
  18.1 6.2 %collective-permute-start.1 = (f32[20,1,8,128]{3,2,1,0:T(8,128)S(1)}, f32[20,1,8,128]{3,2,1,0:T(8,128)S(1)}, u32[]{:S(2)}, u32[]{:S(2)}) collective-permute-start(f32[20,1,8,128]{3,2,1,0:T(8,128)S(1)} %get-tuple-element.97), channel_id=1, source_target_pairs={{4,0},{8,4},{12,8},{16,12},{20,16},{24,20},{28,24},{0,28},{5,1},{9... | collective-permute-start | bytes 245768 | tf_op jit(solution)/shard_map/ppermute | solution.py:56
  24.4 3.5 %collective-permute-start.2 = (f32[20,4,1,128]{3,2,1,0:T(1,128)S(1)}, f32[20,4,1,128]{3,2,1,0:T(1,128)S(1)}, u32[]{:S(2)}, u32[]{:S(2)}) collective-permute-start(f32[20,4,1,128]{3,2,1,0:T(1,128)S(1)} %get-tuple-element.86), channel_id=1, source_target_pairs={{0,1},{1,2},{2,3},{3,0},{4,5},{5,6},{6,7},{7,4},{8,9},{9,10},{10,1... | collective-permute-start | bytes 122888 | tf_op jit(solution)/shard_map/ppermute | solution.py:53
  24.4 3.4 %collective-permute-start.3 = (f32[20,4,1,128]{3,2,1,0:T(1,128)S(1)}, f32[20,4,1,128]{3,2,1,0:T(1,128)S(1)}, u32[]{:S(2)}, u32[]{:S(2)}) collective-permute-start(f32[20,4,1,128]{3,2,1,0:T(1,128)S(1)} %get-tuple-element.87), channel_id=1, source_target_pairs={{1,0},{2,1},{3,2},{0,3},{5,4},{6,5},{7,6},{4,7},{9,8},{10,9},{11,1... | collective-permute-start | bytes 122888 | tf_op jit(solution)/shard_map/ppermute | solution.py:56
  26.9 3.2 copy-start.34
  32.8 14.8 %collective-permute-start.4 = (f32[23,1,8,128]{3,2,1,0:T(8,128)}, f32[23,1,8,128]{3,2,1,0:T(8,128)S(1)}, u32[]{:S(2)}, u32[]{:S(2)}) collective-permute-start(f32[23,1,8,128]{3,2,1,0:T(8,128)} %get-tuple-element.90), channel_id=1, source_target_pairs={{0,4},{4,8},{8,12},{12,16},{16,20},{20,24},{24,28},{28,0},{1,5},{5... | collective-permute-start | bytes 282632 | tf_op jit(solution)/shard_map/ppermute | solution.py:53
  33.5 14.1 %collective-permute-start.5 = (f32[23,1,8,128]{3,2,1,0:T(8,128)}, f32[23,1,8,128]{3,2,1,0:T(8,128)}, u32[]{:S(2)}, u32[]{:S(2)}) collective-permute-start(f32[23,1,8,128]{3,2,1,0:T(8,128)} %get-tuple-element.91), channel_id=1, source_target_pairs={{4,0},{8,4},{12,8},{16,12},{20,16},{24,20},{28,24},{0,28},{5,1},{9... | collective-permute-start | bytes 282632 | tf_op jit(solution)/shard_map/ppermute | solution.py:56
  41.1 2.9 copy-start.107
  49.3 9.5 %collective-permute-start.6 = (f32[23,4,1,128]{3,2,1,0:T(1,128)}, f32[23,4,1,128]{3,2,1,0:T(1,128)S(1)}, u32[]{:S(2)}, u32[]{:S(2)}) collective-permute-start(f32[23,4,1,128]{3,2,1,0:T(1,128)} %get-tuple-element.82), channel_id=1, source_target_pairs={{0,1},{1,2},{2,3},{3,0},{4,5},{5,6},{6,7},{7,4},{8,9},{9,10},{10,1... | collective-permute-start | bytes 141320 | tf_op jit(solution)/shard_map/ppermute | solution.py:53
  50.4 8.5 %collective-permute-start.7 = (f32[23,4,1,128]{3,2,1,0:T(1,128)}, f32[23,4,1,128]{3,2,1,0:T(1,128)}, u32[]{:S(2)}, u32[]{:S(2)}) collective-permute-start(f32[23,4,1,128]{3,2,1,0:T(1,128)} %get-tuple-element.83), channel_id=1, source_target_pairs={{1,0},{2,1},{3,2},{0,3},{5,4},{6,5},{7,6},{4,7},{9,8},{10,9},{11,1... | collective-permute-start | bytes 141320 | tf_op jit(solution)/shard_map/ppermute | solution.py:56
  81.3 2.8 copy-start.9
  81.3 2.8 copy-start.25
  81.3 2.8 copy-start.66
  89.0 4.5 %copy-start.65 = (f32[2,8,127]{2,1,0:T(8,128)S(1)}, f32[2,8,127]{2,1,0:T(8,128)}, u32[]{:S(2)}) copy-start(f32[2,8,127]{2,1,0:T(8,128)} %copy-done.64) | copy-start | bytes 24388
  89.0 4.5 %copy-start.63 = (f32[2,8,127]{2,1,0:T(8,128)S(1)}, f32[2,8,127]{2,1,0:T(8,128)}, u32[]{:S(2)}) copy-start(f32[2,8,127]{2,1,0:T(8,128)} %copy-done.62) | copy-start | bytes 24388
  89.0 7.4 %copy-start.55 = (f32[2,8,127]{2,1,0:T(8,128)S(1)}, f32[2,8,127]{2,1,0:T(8,128)}, u32[]{:S(2)}) copy-start(f32[2,8,127]{2,1,0:T(8,128)} %copy-done.54) | copy-start | bytes 24388
  90.5 10.7 %copy-start.12 = (f32[19,2,8,128]{3,2,1,0:T(8,128)S(1)}, f32[19,2,8,128]{3,2,1,0:T(8,128)}, u32[]{:S(2)}) copy-start(f32[19,2,8,128]{3,2,1,0:T(8,128)} %gather_fusion.2) | copy-start | bytes 466948
  106.7 4.8 %copy-start.29 = (f32[19,128]{1,0:T(8,128)S(1)}, f32[19,128]{1,0:T(8,128)}, u32[]{:S(2)}) copy-start(f32[19,128]{1,0:T(8,128)} %param.29) | copy-start | bytes 29188
  106.8 7.2 %collective-permute-start.8 = (f32[20,1,8,128]{3,2,1,0:T(8,128)S(1)}, f32[20,1,8,128]{3,2,1,0:T(8,128)S(1)}, u32[]{:S(2)}, u32[]{:S(2)}) collective-permute-start(f32[20,1,8,128]{3,2,1,0:T(8,128)S(1)} %get-tuple-element.94), channel_id=1, source_target_pairs={{0,4},{4,8},{8,12},{12,16},{16,20},{20,24},{24,28},{28,0},{1,5},{5... | collective-permute-start | bytes 245768 | tf_op jit(solution)/shard_map/ppermute | solution.py:53
  106.8 7.1 %collective-permute-start.9 = (f32[20,1,8,128]{3,2,1,0:T(8,128)S(1)}, f32[20,1,8,128]{3,2,1,0:T(8,128)S(1)}, u32[]{:S(2)}, u32[]{:S(2)}) collective-permute-start(f32[20,1,8,128]{3,2,1,0:T(8,128)S(1)} %get-tuple-element.95), channel_id=1, source_target_pairs={{4,0},{8,4},{12,8},{16,12},{20,16},{24,20},{28,24},{0,28},{5,1},{9... | collective-permute-start | bytes 245768 | tf_op jit(solution)/shard_map/ppermute | solution.py:56
  114.0 3.5 %collective-permute-start.10 = (f32[20,4,1,128]{3,2,1,0:T(1,128)S(1)}, f32[20,4,1,128]{3,2,1,0:T(1,128)S(1)}, u32[]{:S(2)}, u32[]{:S(2)}) collective-permute-start(f32[20,4,1,128]{3,2,1,0:T(1,128)S(1)} %get-tuple-element.84), channel_id=1, source_target_pairs={{0,1},{1,2},{2,3},{3,0},{4,5},{5,6},{6,7},{7,4},{8,9},{9,10},{10,1... | collective-permute-start | bytes 122888 | tf_op jit(solution)/shard_map/ppermute | solution.py:53
  114.1 3.4 %collective-permute-start.11 = (f32[20,4,1,128]{3,2,1,0:T(1,128)S(1)}, f32[20,4,1,128]{3,2,1,0:T(1,128)S(1)}, u32[]{:S(2)}, u32[]{:S(2)}) collective-permute-start(f32[20,4,1,128]{3,2,1,0:T(1,128)S(1)} %get-tuple-element.85), channel_id=1, source_target_pairs={{1,0},{2,1},{3,2},{0,3},{5,4},{6,5},{7,6},{4,7},{9,8},{10,9},{11,1... | collective-permute-start | bytes 122888 | tf_op jit(solution)/shard_map/ppermute | solution.py:56
  121.3 7.4 %collective-permute-start.12 = (f32[23,1,8,128]{3,2,1,0:T(8,128)S(1)}, f32[23,1,8,128]{3,2,1,0:T(8,128)S(1)}, u32[]{:S(2)}, u32[]{:S(2)}) collective-permute-start(f32[23,1,8,128]{3,2,1,0:T(8,128)S(1)} %get-tuple-element.88), channel_id=1, source_target_pairs={{0,4},{4,8},{8,12},{12,16},{16,20},{20,24},{24,28},{28,0},{1,5},{5... | collective-permute-start | bytes 282632 | tf_op jit(solution)/shard_map/ppermute | solution.py:53
  121.3 7.3 %collective-permute-start.13 = (f32[23,1,8,128]{3,2,1,0:T(8,128)S(1)}, f32[23,1,8,128]{3,2,1,0:T(8,128)S(1)}, u32[]{:S(2)}, u32[]{:S(2)}) collective-permute-start(f32[23,1,8,128]{3,2,1,0:T(8,128)S(1)} %get-tuple-element.89), channel_id=1, source_target_pairs={{4,0},{8,4},{12,8},{16,12},{20,16},{24,20},{28,24},{0,28},{5,1},{9... | collective-permute-start | bytes 282632 | tf_op jit(solution)/shard_map/ppermute | solution.py:56
  128.8 3.8 %collective-permute-start.14 = (f32[23,4,1,128]{3,2,1,0:T(1,128)S(1)}, f32[23,4,1,128]{3,2,1,0:T(1,128)S(1)}, u32[]{:S(2)}, u32[]{:S(2)}) collective-permute-start(f32[23,4,1,128]{3,2,1,0:T(1,128)S(1)} %get-tuple-element.80), channel_id=1, source_target_pairs={{0,1},{1,2},{2,3},{3,0},{4,5},{5,6},{6,7},{7,4},{8,9},{9,10},{10,1... | collective-permute-start | bytes 141320 | tf_op jit(solution)/shard_map/ppermute | solution.py:53
  129.6 3.3 %collective-permute-start.15 = (f32[23,4,1,128]{3,2,1,0:T(1,128)S(1)}, f32[23,4,1,128]{3,2,1,0:T(1,128)S(1)}, u32[]{:S(2)}, u32[]{:S(2)}) collective-permute-start(f32[23,4,1,128]{3,2,1,0:T(1,128)S(1)} %get-tuple-element.81), channel_id=1, source_target_pairs={{1,0},{2,1},{3,2},{0,3},{5,4},{6,5},{7,6},{4,7},{9,8},{10,9},{11,1... | collective-permute-start | bytes 141320 | tf_op jit(solution)/shard_map/ppermute | solution.py:56
  145.7 3.2 copy-start.67
  205.7 113.6 %copy-start.15 = (f32[19,2,8,128]{3,2,1,0:T(8,128)}, f32[19,2,8,128]{3,2,1,0:T(8,128)S(1)}, u32[]{:S(2)}) copy-start(f32[19,2,8,128]{3,2,1,0:T(8,128)S(1)} %scatter_fusion.1) | copy-start | bytes 466948
  (99 other events, 116.7 us)
Sparse Core Ops, SparseCore 0:
  199.8 117.9 all-reduce.40
where the time goes:
time: 330 us; the launch traced here: 326 us
  waiting for transfers between devices  119 us (36%)
  local copies, waits for them, and re-layouts  70.1 us (21%)
  blocking collectives  40.7 us (12%)
  matrix products  29.2 us (9%)
  starting transfers between devices  28.1 us (9%)
  other arithmetic  23 us (7%)
  between operations  15.6 us (5%)
    psum x1, waiting for transfers between devices, per_device(): lax.psum((accumulated[0], accumulated[1], accumulated[2], accumulated[3],...  112 us
    psum x1, blocking collectives, per_device(): lax.psum((accumulated[0], accumulated[1], accumulated[2], accumulated[3],...  40.7 us
    unnamed x294, local copies, waits for them, and re-layouts  27.3 us
    ppermute x8, starting transfers between devices, with_halo(): lax.ppermute(lax.slice_in_dim(block, 0, width, axis=dim), axis, backward)  22.3 us
    slice x27, local copies, waits for them, and re-layouts, stream_pull(): planes[i]  10.8 us
    dot_general x6, matrix products, collide(): lax.dot_general(exit_level_matrix, hidden_two, CONTRACT, precision=PRECIS...  10.3 us
    dot_general x6, matrix products, collide(): lax.dot_general(inner_level_matrix, hidden_one, CONTRACT, precision=PRECI...  9.83 us
    another operation x6, local copies, waits for them, and re-layouts, stream_pull(): return jnp.stack(pulled)  8.3 us
  transfers between devices with their start and end apart: 17, of which 8 were waited for; matrix products, arithmetic and copies ran while one was open for 8% of the time, Pallas kernels for 0%

commit v1 on v0

v1 whole, which is shorter than its diff:
```python
import functools
import math

import jax
import jax.numpy as jnp
import numpy as np
from jax import lax
from jax.experimental import pallas as pl
from jax.experimental.pallas import tpu as pltpu
from jax.sharding import PartitionSpec as P

VELOCITIES = np.array(
    [
        [0, 0, 0],
        [1, 0, 0],
        [-1, 0, 0],
        [0, 1, 0],
        [0, -1, 0],
        [0, 0, 1],
        [0, 0, -1],
        [1, 1, 0],
        [-1, -1, 0],
        [1, -1, 0],
        [-1, 1, 0],
        [1, 0, 1],
        [-1, 0, -1],
        [1, 0, -1],
        [-1, 0, 1],
        [0, 1, 1],
        [0, -1, -1],
        [0, 1, -1],
        [0, -1, 1],
    ]
)
Q = len(VELOCITIES)
OPPOSITE = [0, 2, 1, 4, 3, 6, 5, 8, 7, 10, 9, 12, 11, 14, 13, 16, 15, 18, 17]
LATTICE_WEIGHTS = np.array([1.0 / 3.0] + [1.0 / 18.0] * 6 + [1.0 / 36.0] * 12)
BUOYANCY = [float(v) for v in 0.3 * LATTICE_WEIGHTS * VELOCITIES[:, 2]]
CONDUCTIVITY = 0.1
HOT_WALL = 0.5
COLD_WALL = -0.5
HEATER = 0.5
SIGNS = (1, -1)
CORNERS = [(1, 1), (1, -1), (-1, 1), (-1, -1)]
LANES = 128
ROWS = 32
SLOTS = 6
MESH = pl.DeviceIdType.MESH
BF16 = jnp.bfloat16
F32 = jnp.float32
NN = (((1,), (0,)), ((), ()))
NT = (((1,), (1,)), ((), ()))


def steps_of(orient):
    return [tuple(int(v) * orient for v in VELOCITIES[i]) for i in range(Q)]


def movers(orient, axis, sign):
    return [i for i, step in enumerate(steps_of(orient)) if step[axis] == sign]


def corner_mover(orient, dx, dy):
    return steps_of(orient).index((dx, dy, 0))


def halves(values):
    high = values.astype(BF16)
    return high, (values - high.astype(F32)).astype(BF16)


def dot(a, b, dims):
    return lax.dot_general(a, b, dims, preferred_element_type=F32)


def kernel(
    sizes,
    f0, t0, site, w1, b1, w2, b2, w3, b3, adj2, tadj2,
    adj_out, tadj_out, gw1, gb1, gw2, gb2, gw3, gb3,
    post, f1, t1, adj1, tadj1, net, pcg, pcgf,
    ft, pt, h1, h2, h1c, h2c, d1c, d2c,
    square, m1, m2, m3, r1, r2, r3, col,
    sx, sy, sc, rx, ry, rc, send, recv,
    grads, parts_y, parts_x, total, gsend, grecv,
):
    nx, ny, nz, ngx, ngy, factor = sizes
    cols = nx * ny
    sites = cols * nz
    hid = w2.shape[0]
    chunk = min(4, cols)
    gx, gy = lax.axis_index("gx"), lax.axis_index("gy")

    def device(dx, dy):
        return (lax.rem(gx + dx + ngx, ngx), lax.rem(gy + dy + ngy, ngy))

    barrier = pltpu.get_barrier_semaphore()
    partners = [(d, 0) for d in range(1, ngx)] + [(0, d) for d in range(1, ngy)] + CORNERS
    for dx, dy in partners:
        pl.semaphore_signal(barrier, inc=1, device_id=device(dx, dy), device_id_type=MESH)

    def rows(i, x):
        return pl.ds((i * nx + x) * ny, ny)

    def row(i, x, y):
        return pl.ds((i * nx + x) * ny + y, 1)

    depth = lax.broadcasted_iota(jnp.int32, (ny, nz), 1)
    height = lax.broadcasted_iota(jnp.int32, (ny, nz), 0)

    square[...] = jnp.zeros_like(square)
    square[0:Q, :] = w1[...]
    square[Q : Q + 1, :] = b1[...]
    w1_rows = square[...]
    a, b = halves(jnp.transpose(w1_rows)[:, :ROWS])
    m1[...] = jnp.concatenate([a, a, b], axis=1)
    a, b = halves(w1_rows[:ROWS])
    r1[...] = jnp.concatenate(
        [jnp.concatenate([a, a], axis=1), jnp.concatenate([b, jnp.zeros_like(b)], axis=1)], axis=0
    )
    for matrix, target in ((jnp.transpose(w2[...]), m2), (w2[...], r2)):
        a, b = halves(matrix)
        target[...] = jnp.concatenate(
            [jnp.concatenate([a, a], axis=1), jnp.concatenate([b, jnp.zeros_like(b)], axis=1)],
            axis=0,
        )
    square[...] = jnp.zeros_like(square)
    square[:, 0:Q] = w3[...]
    w3_cols = square[...]
    a, b = halves(jnp.transpose(w3_cols)[:ROWS])
    m3[...] = jnp.concatenate(
        [jnp.concatenate([a, a], axis=1), jnp.concatenate([b, jnp.zeros_like(b)], axis=1)], axis=0
    )
    a, b = halves(w3_cols[:, :ROWS])
    r3[...] = jnp.concatenate([a, a, b], axis=1)
    square[...] = jnp.zeros_like(square)
    square[0:1, :] = b2[...]
    square[1:2, 0:Q] = b3[...]
    col[...] = jnp.transpose(square[...])

    for s in range(2):
        ft[s] = jnp.zeros((ROWS, sites), F32)
        ft[s, Q : Q + 1, :] = jnp.ones((1, sites), F32)
    pt[...] = jnp.zeros_like(pt)

    def to_rows(source, target):
        for c in range(cols):
            target[0:Q, c * nz : (c + 1) * nz] = source[pl.ds(c, Q, stride=cols), :]

    def to_planes(values, first, target):
        for c in range(chunk):
            target[pl.ds(first + c, Q, stride=cols), :] = values[0:Q, c * nz : (c + 1) * nz]

    def chunks():
        for first in range(0, cols, chunk):
            yield first, pl.ds(first * nz, chunk * nz)

    def hidden(s, at):
        a, b = halves(ft[s, :, at])
        one = jnp.tanh(dot(m1[...], jnp.concatenate([a, b, a], axis=0), NN))
        h1[s, :, at] = one
        pair = jnp.concatenate(halves(one), axis=0)
        h1c[s, :, at] = pair
        both = dot(m2[...], pair, NN)
        two = jnp.tanh(both[:hid] + both[hid:] + col[:, 0:1])
        h2[s, :, at] = two
        pair = jnp.concatenate(halves(two), axis=0)
        h2c[s, :, at] = pair
        return pair

    def network_back(s, first, at):
        a, b = halves(pt[s, :, at])
        back = dot(r3[...], jnp.concatenate([a, b, a], axis=0), NN)
        two = h2[s, :, at]
        pair = jnp.concatenate(halves(back * (1.0 - two * two)), axis=0)
        d2c[s, :, at] = pair
        both = dot(r2[...], pair, NN)
        one = h1[s, :, at]
        pair = jnp.concatenate(halves((both[:hid] + both[hid:]) * (1.0 - one * one)), axis=0)
        d1c[s, :, at] = pair
        both = dot(r1[...], pair, NN)
        to_planes(both[:ROWS] + both[ROWS:], first, net)

    def folded(product, n, m):
        return product[:n, :m] + product[:n, m : 2 * m] + product[n : 2 * n, :m]

    at1, at2 = 0, ROWS
    at3 = at2 + hid
    at4 = at3 + 8
    at5 = at4 + ROWS

    def weight_grads(s):
        pairs = dot(jnp.concatenate(halves(ft[s]), axis=0), d1c[s], NT)
        first = folded(pairs, ROWS, hid)
        ones = jnp.ones((16, sites), BF16)
        pairs = dot(jnp.concatenate([h1c[s], ones], axis=0), d2c[s], NT)
        second = folded(pairs, hid, hid)
        second_bias = pairs[2 * hid : 2 * hid + 8, :hid] + pairs[2 * hid : 2 * hid + 8, hid:]
        pairs = dot(jnp.concatenate(halves(pt[s]), axis=0), h2c[s], NT)
        third = folded(pairs, ROWS, hid)
        third_bias = jnp.broadcast_to(jnp.sum(pt[s], axis=1, keepdims=True), (ROWS, LANES))
        for start, value in (
            (at1, first), (at2, second), (at3, second_bias), (at4, third), (at5, third_bias)
        ):
            where = pl.ds(start, value.shape[0])
            if s == 1:
                grads[where, :] = value
            else:
                grads[where, :] = (grads[where, :] + value) * factor

    started = []

    def begin(e, source, orient, extras, corners):
        found = {}
        for k, sign in enumerate(SIGNS):
            slot = 0
            for i in movers(orient, 0, sign) if source is not None else ():
                sx[e, k, slot * ny : (slot + 1) * ny, :] = source[
                    rows(i, nx - 1 if sign == 1 else 0), :
                ]
                slot += 1
            for extra in extras:
                sx[e, k, slot * ny : (slot + 1) * ny, :] = extra(
                    0, sign, nx - 1 if sign == 1 else 0
                )
                slot += 1
            slot = 0
            edge = ny - 1 if sign == 1 else 0
            for i in movers(orient, 1, sign) if source is not None else ():
                for x in range(nx):
                    sy[e, k, slot * nx + x : slot * nx + x + 1, :] = source[row(i, x, edge), :]
                slot += 1
            for extra in extras:
                for x in range(nx):
                    sy[e, k, slot * nx + x : slot * nx + x + 1, :] = extra(1, sign, x)[
                        edge : edge + 1, :
                    ]
                slot += 1
        if corners:
            for k, (dx, dy) in enumerate(CORNERS):
                i = corner_mover(orient, dx, dy)
                sc[e, k, 0:1, :] = source[
                    row(i, nx - 1 if dx == 1 else 0, ny - 1 if dy == 1 else 0), :
                ]

        def copy(src, dst, n, dx, dy):
            found[n] = pltpu.make_async_remote_copy(
                src_ref=src, dst_ref=dst, send_sem=send.at[e, n], recv_sem=recv.at[e, n],
                device_id=device(dx, dy), device_id_type=MESH,
            )
            found[n].start()

        for k, sign in enumerate(SIGNS):
            copy(sx.at[e, k], rx.at[e, k], k, sign, 0)
            copy(sy.at[e, k], ry.at[e, k], 2 + k, 0, sign)
        if corners:
            for k, (dx, dy) in enumerate(CORNERS):
                copy(sc.at[e, k], rc.at[e, k], 4 + k, dx, dy)
        started.extend(found.values())
        return list(found.values())

    def arrive(copies):
        for c in copies:
            c.wait_recv()

    def moved_x(inside, e, slot, x, sign):
        if 0 <= x - sign < nx:
            return inside(x - sign)
        return rx[e, SIGNS.index(sign), slot * ny : (slot + 1) * ny, :]

    def moved_y(plane, edge_row, sign):
        shifted = pltpu.roll(plane, 1 if sign == 1 else ny - 1, 0)
        edge = 0 if sign == 1 else ny - 1
        return jnp.where(height == edge, jnp.broadcast_to(edge_row, shifted.shape), shifted)

    def moved_z(plane, fill, sign):
        shifted = pltpu.roll(plane, 1 if sign == 1 else nz - 1, 1)
        return jnp.where(depth == (0 if sign == 1 else nz - 1), fill, shifted)

    def face_y(e, slot, x, sign):
        at = slot * nx + x
        return ry[e, SIGNS.index(sign), at : at + 1, :]

    def stream(source, e, orient, store):
        for i, (px, py, pz) in enumerate(steps_of(orient)):
            for x in range(nx):
                plane = None
                if px:
                    plane = moved_x(
                        lambda k: source[rows(i, k), :],
                        e, movers(orient, 0, px).index(i), x, px,
                    )
                else:
                    plane = source[rows(i, x), :]
                if py:
                    if 0 <= x - px < nx:
                        edge = face_y(e, movers(orient, 1, py).index(i), x - px, py)
                    else:
                        edge = rc[e, CORNERS.index((px, py)), 0:1, :]
                    plane = moved_y(plane, edge, py)
                if pz:
                    plane = moved_z(plane, source[rows(OPPOSITE[i], x), :], pz)
                store(i, x, plane)

    def motion(fields, x):
        result = []
        for a in range(3):
            value = None
            for i in range(Q):
                if VELOCITIES[i, a] == 0:
                    continue
                term = fields[rows(i, x), :]
                if value is None:
                    value = term if VELOCITIES[i, a] == 1 else -term
                elif VELOCITIES[i, a] == 1:
                    value = value + term
                else:
                    value = value - term
            result.append(value)
        return result

    def heat_near(field, e, slot, x, a, s):
        if a == 0:
            return moved_x(lambda k: field[k], e, slot, x, -s)
        if a == 1:
            return moved_y(field[x], face_y(e, slot, x, -s), -s)
        return moved_z(field[x], COLD_WALL if s == 1 else HOT_WALL, -s)

    def fluid(x):
        return site[x] == 0

    def liquid(tadj, x):
        return jnp.where(fluid(x), tadj[x], 0.0)

    def flux(fields, tadj, x, a, s):
        return (CONDUCTIVITY - 0.5 * s * motion(fields, x)[a]) * liquid(tadj, x)

    to_rows(f0, ft.at[0])
    for first, at in chunks():
        pair = hidden(0, at)
        both = dot(m3[...], pair, NN)
        to_planes(both[:ROWS] + both[ROWS:] + col[:ROWS, 1:2], first, net)
    for x in range(nx):
        open_cell = fluid(x)
        for i in range(Q):
            value = f0[rows(i, x), :] + net[rows(i, x), :]
            if BUOYANCY[i] != 0.0:
                value = value + BUOYANCY[i] * t0[x]
            post[rows(i, x), :] = jnp.where(open_cell, value, f0[rows(OPPOSITE[i], x), :])
    pl.semaphore_wait(barrier, len(partners))
    copies_a = begin(0, post, 1, [lambda a, s, x: t0[x]], True)
    copies_0 = begin(1, adj2, -1, [], True)
    speeds0 = [motion(f0, x) for x in range(nx)]
    arrive(copies_a)

    def keep_f1(i, x, plane):
        f1[rows(i, x), :] = plane

    stream(post, 0, 1, keep_f1)
    for x in range(nx):
        value = (1.0 - 6.0 * CONDUCTIVITY) * t0[x]
        for a in range(3):
            for s in SIGNS:
                value = value + (CONDUCTIVITY - 0.5 * s * speeds0[x][a]) * heat_near(
                    t0, 0, 5, x, a, s
                )
        t1[x] = jnp.where(fluid(x), value, jnp.where(site[x] == 1, t0[x], HEATER))
    copies_b = begin(
        2, None, 1,
        [lambda a, s, x: t1[x], lambda a, s, x: flux(f1, tadj2, x, a, s)], False,
    )

    to_rows(f1, ft.at[1])
    for first, at in chunks():
        hidden(1, at)

    def step_back(s, fields, field, adjoint, tadj, e_adj, e_heat, heat_slot, e_flux, flux_slot,
                  waits, new_adj, new_tadj):
        lifts = [jnp.zeros((ny, nz), F32) for _ in range(nx)]

        def keep(i, x, plane):
            pcg[rows(i, x), :] = plane
            value = jnp.where(fluid(x), plane, 0.0)
            pcgf[rows(i, x), :] = value
            if BUOYANCY[i] != 0.0:
                lifts[x] = lifts[x] + BUOYANCY[i] * value

        stream(adjoint, e_adj, -1, keep)
        to_rows(pcgf, pt.at[s])
        for first, at in chunks():
            network_back(s, first, at)
        arrive(waits)
        for x in range(nx):
            wet = liquid(tadj, x)
            speed = motion(fields, x)
            value = (1.0 - 6.0 * CONDUCTIVITY) * wet + jnp.where(site[x] == 1, tadj[x], 0.0)
            for a in range(3):
                for sign in SIGNS:
                    if a == 0:
                        value = value + moved_x(
                            lambda k: flux(fields, tadj, k, 0, sign), e_flux, flux_slot, x, sign
                        )
                        continue
                    here = (CONDUCTIVITY - 0.5 * sign * speed[a]) * wet
                    if a == 1:
                        value = value + moved_y(here, face_y(e_flux, flux_slot, x, sign), sign)
                    else:
                        value = value + moved_z(here, 0.0, sign)
            new_tadj[x] = value + lifts[x]
            pulls = [
                wet * (0.5 * (heat_near(field, e_heat, heat_slot, x, a, -1)
                              - heat_near(field, e_heat, heat_slot, x, a, 1)))
                for a in range(3)
            ]
            open_cell = fluid(x)
            for i in range(Q):
                value = net[rows(i, x), :] + jnp.where(
                    open_cell, pcg[rows(i, x), :], pcg[rows(OPPOSITE[i], x), :]
                )
                for a in range(3):
                    if VELOCITIES[i, a] == 1:
                        value = value + pulls[a]
                    elif VELOCITIES[i, a] == -1:
                        value = value - pulls[a]
                new_adj[rows(i, x), :] = value

    arrive(copies_0)
    step_back(1, f1, t1, adj2, tadj2, 1, 2, 0, 2, 1, copies_b, adj1, tadj1)
    copies_c = begin(3, adj1, -1, [lambda a, s, x: flux(f0, tadj1, x, a, s)], True)
    weight_grads(1)
    arrive(copies_c)
    step_back(0, f0, t0, adj1, tadj1, 3, 0, 5, 3, 5, [], adj_out, tadj_out)
    weight_grads(0)

    part = grads.shape[0] // ngy
    if at5 + ROWS < grads.shape[0]:
        grads[at5 + ROWS :, :] = jnp.zeros((grads.shape[0] - at5 - ROWS, LANES), F32)

    def block(index):
        return pl.ds(pl.multiple_of(index * part, 8), part)

    def share(src, dst, n, dx, dy):
        c = pltpu.make_async_remote_copy(
            src_ref=src, dst_ref=dst, send_sem=gsend.at[n], recv_sem=grecv.at[n],
            device_id=device(dx, dy), device_id_type=MESH,
        )
        c.start()
        started.append(c)
        return c

    copies = []
    for d in range(1, ngy):
        copies.append(
            share(grads.at[block(lax.rem(gy + d, ngy))], parts_y.at[d - 1], d - 1, 0, d)
        )
    value = grads[block(gy), :]
    arrive(copies)
    for d in range(1, ngy):
        value = value + parts_y[d - 1]
    parts_x[0] = value
    copies = []
    for d in range(1, ngx):
        copies.append(share(parts_x.at[0], parts_x.at[d], ngy - 1 + d - 1, d, 0))
    arrive(copies)
    value = None
    for k in range(ngx):
        term = parts_x[lax.rem(gx - k + ngx, ngx)]
        value = term if value is None else value + term
    total[block(gy), :] = value
    copies = []
    for d in range(1, ngy):
        copies.append(
            share(total.at[block(gy)], total.at[block(gy)], ngy + ngx - 2 + d - 1, 0, d)
        )
    arrive(copies)
    gw1[...] = total[at1 : at1 + Q, :]
    gb1[...] = total[at1 + Q : at1 + Q + 1, :]
    gw2[...] = total[at2 : at2 + hid, :]
    gb2[...] = total[at3 : at3 + 1, :]
    square[...] = jnp.zeros_like(square)
    square[0:ROWS, :] = total[at4 : at4 + ROWS, :]
    gw3[...] = jnp.transpose(square[...])[:, 0:Q]
    square[0:ROWS, :] = total[at5 : at5 + ROWS, :]
    gb3[...] = jnp.transpose(square[...])[0:1, 0:Q]
    for c in started:
        c.wait_send()


def per_device(ngx, ngy, f0, t0, site, w1, b1, w2, b2, w3, b3, adj2, tadj2):
    q, nx, ny, nz = f0.shape
    hid = w2.shape[0]
    sites = nx * ny * nz
    flat = (q * nx * ny, nz)
    factor = 1.0 / math.sqrt(nx * ngx * ny * ngy * nz)
    needed = 3 * ROWS + hid + 8
    unit = 8 * ngy
    length = -(-needed // unit) * unit
    side = -(-(SLOTS * nx) // 8) * 8
    plane = pltpu.VMEM((nx, ny, nz), F32)
    wide = pltpu.VMEM(flat, F32)
    dma = pltpu.SemaphoreType.DMA
    gcount = 2 * (ngy - 1) + ngx - 1
    scratch = [
        wide, wide, plane, wide, plane, wide, wide, wide,
        pltpu.VMEM((2, ROWS, sites), F32),
        pltpu.VMEM((2, ROWS, sites), F32),
        pltpu.VMEM((2, hid, sites), F32),
        pltpu.VMEM((2, hid, sites), F32),
        pltpu.VMEM((2, 2 * hid, sites), BF16),
        pltpu.VMEM((2, 2 * hid, sites), BF16),
        pltpu.VMEM((2, 2 * hid, sites), BF16),
        pltpu.VMEM((2, 2 * hid, sites), BF16),
        pltpu.VMEM((hid, hid), F32),
        pltpu.VMEM((hid, 3 * ROWS), BF16),
        pltpu.VMEM((2 * hid, 2 * hid), BF16),
        pltpu.VMEM((2 * ROWS, 2 * hid), BF16),
        pltpu.VMEM((2 * ROWS, 2 * hid), BF16),
        pltpu.VMEM((2 * hid, 2 * hid), BF16),
        pltpu.VMEM((hid, 3 * ROWS), BF16),
        pltpu.VMEM((hid, hid), F32),
        pltpu.VMEM((4, 2, SLOTS * ny, nz), F32),
        pltpu.VMEM((4, 2, side, nz), F32),
        pltpu.VMEM((4, 4, 8, nz), F32),
        pltpu.VMEM((4, 2, SLOTS * ny, nz), F32),
        pltpu.VMEM((4, 2, side, nz), F32),
        pltpu.VMEM((4, 4, 8, nz), F32),
        dma((4, 8)),
        dma((4, 8)),
        pltpu.VMEM((length, LANES), F32),
        pltpu.VMEM((ngy - 1, length // ngy, LANES), F32),
        pltpu.VMEM((ngx, length // ngy, LANES), F32),
        pltpu.VMEM((length, LANES), F32),
        dma((gcount,)),
        dma((gcount,)),
    ]
    shape = jax.ShapeDtypeStruct
    vmem = pl.BlockSpec(memory_space=pltpu.VMEM)
    outs = pl.pallas_call(
        functools.partial(kernel, (nx, ny, nz, ngx, ngy, factor)),
        out_shape=[
            shape(flat, F32), shape((nx, ny, nz), F32),
            shape(w1.shape, F32), shape((1, hid), F32),
            shape(w2.shape, F32), shape((1, hid), F32),
            shape(w3.shape, F32), shape((1, q), F32),
        ],
        in_specs=[vmem] * 11,
        out_specs=[vmem] * 8,
        scratch_shapes=scratch,
        compiler_params=pltpu.CompilerParams(
            collective_id=0, has_side_effects=True, vmem_limit_bytes=48 * 1024 * 1024
        ),
    )(
        f0.reshape(flat), t0, site, w1, b1.reshape(1, hid), w2, b2.reshape(1, hid),
        w3, b3.reshape(1, q), adj2.reshape(flat), tadj2,
    )
    return (
        outs[0].reshape(f0.shape), outs[1], outs[2], outs[3].reshape(hid),
        outs[4], outs[5].reshape(hid), outs[6], outs[7].reshape(q),
    )


def solution(mesh):
    grid = P(None, "gx", "gy", None)
    plane = P("gx", "gy", None)
    in_specs = (grid, plane, plane) + (P(),) * 6 + (grid, plane)
    out_specs = (grid, plane) + (P(),) * 6
    return jax.shard_map(
        functools.partial(per_device, mesh.shape["gx"], mesh.shape["gy"]),
        mesh=mesh, in_specs=in_specs, out_specs=out_specs, check_vma=False,
    )
```

time: 330 us -> 44.9 us (0.14); the launches traced: 326 us -> 44.6 us
  waiting for transfers between devices: 119 us -> 0 us
  local copies, waits for them, and re-layouts: 70.1 us -> 9.44 us
  blocking collectives: 40.7 us -> 0 us
  Pallas kernels: 0 us -> 34.4 us
  matrix products: 29.2 us -> 0 us
  starting transfers between devices: 28.1 us -> 0 us
  other arithmetic: 23 us -> 0 us
  between operations: 15.6 us -> 0.73 us
    psum x1 -> x0, waiting for transfers between devices: 112 us -> none  [per_device(): lax.psum((accumulated[0], accumulated[1], accumulated[2], accumulated[3],...]
    psum x1 -> x0, blocking collectives: 40.7 us -> none  [per_device(): lax.psum((accumulated[0], accumulated[1], accumulated[2], accumulated[3],...]
    pallas_call x0 -> x1, Pallas kernels: none -> 34.4 us  [per_device(): pl.pallas_call(functools.partial(kernel, (nx, ny, nz, ngx, ngy, factor)),...]
    dot_general x22 -> x0, matrix products: 29.2 us -> none  [the longest x6 10.3 us: collide(): lax.dot_general(exit_level_matrix, hidden_two, CONTRACT, precision=PRECIS...]
    ppermute x16 -> x0, starting transfers between devices: 28.1 us -> none  [the longest x8 22.3 us: with_halo(): lax.ppermute(lax.slice_in_dim(block, 0, width, axis=dim), axis, backward)]
    unnamed x294 -> x29, local copies, waits for them, and re-layouts: 27.3 us -> 9.44 us
    slice x61 -> x0, local copies, waits for them, and re-layouts: 13.3 us -> none  [the longest x27 10.8 us: stream_pull(): planes[i]]
    pad x30 -> x0, local copies, waits for them, and re-layouts: 13.1 us -> none  [the longest x15 7.05 us: propagation_offset(): return jnp.pad(window[..., :-1], lead + [(1, 0)])]
  transfers between devices with their start and end apart: 17 -> 0, of which waited for: 8 -> 0; matrix products, arithmetic and copies ran while one was open for 8% -> 0% of each run, Pallas kernels for 0% -> 0%
where the time goes in v1:
time: 44.9 us; the launch traced here: 44.6 us
  Pallas kernels  34.4 us (77%)
  local copies, waits for them, and re-layouts  9.44 us (21%)
  between operations  0.73 us (2%)
    pallas_call x1, Pallas kernels, per_device(): pl.pallas_call(functools.partial(kernel, (nx, ny, nz, ngx, ngy, factor)),...  34.4 us
    unnamed x29, local copies, waits for them, and re-layouts  9.44 us

profile of v1, /device:TPU:0, one launch (start us, length us, event | category | flops | bytes accessed | tf_op | source)
XLA Modules:
  0.0 44.6 jit_solution(9809140344257556302)
XLA Ops:
  0.6 0.0 copy-start.2
  0.6 0.0 copy-start.3
  0.7 0.0 copy-start.4
  0.7 0.0 copy-start.7
  0.7 0.0 copy-start.8
  0.7 0.9 %copy.19.w3 = f32[128,19]{1,0:T(8,128)S(1)} copy(f32[128,19]{0,1:T(8,128)} %param.18) | data formatting | bytes 19456 | tf_op args[7]
  1.5 0.0 copy-done.2
  1.5 0.0 copy-done.3
  1.6 0.0 copy-done.4
  1.6 0.0 copy-done.7
  1.6 0.0 copy-done.8
  1.6 0.0 copy-start
  1.6 0.9 %copy-done = f32[19,2,8,128]{3,2,1,0:T(8,128)S(1)} copy-done((f32[19,2,8,128]{3,2,1,0:T(8,128)S(1)}, f32[19,2,8,128]{3,2,1,0:T(8,128)}, u32[]{:S(2)}) %copy-start) | copy-done | bytes 155672
  2.5 0.0 copy-start.1
  2.5 0.9 %copy-done.1 = f32[19,2,8,128]{3,2,1,0:T(8,128)S(1)} copy-done((f32[19,2,8,128]{3,2,1,0:T(8,128)S(1)}, f32[19,2,8,128]{3,2,1,0:T(8,128)}, u32[]{:S(2)}) %copy-start.1) | copy-done | bytes 155672
  3.4 0.0 copy-start.5
  3.4 0.7 %copy-done.5 = s32[2,8,128]{2,1,0:T(8,128)S(1)} copy-done((s32[2,8,128]{2,1,0:T(8,128)S(1)}, s32[2,8,128]{2,1,0:T(8,128)}, u32[]{:S(2)}) %copy-start.5) | copy-done | bytes 8216
  4.1 0.0 copy-start.6
  4.1 0.7 %copy-done.6 = f32[2,8,128]{2,1,0:T(8,128)S(1)} copy-done((f32[2,8,128]{2,1,0:T(8,128)S(1)}, f32[2,8,128]{2,1,0:T(8,128)}, u32[]{:S(2)}) %copy-start.6) | copy-done | bytes 8216
  4.8 0.0 copy-start.9
  4.8 0.7 %copy-done.9 = f32[19]{0:T(128)S(1)} copy-done((f32[19]{0:T(128)S(1)}, f32[19]{0:T(128)}, u32[]{:S(2)}) %copy-start.9) | copy-done | bytes 100
  5.5 34.4 %shard_map.170 = (f32[304,128]{1,0:T(8,128)S(1)}, f32[2,8,128]{2,1,0:T(8,128)S(1)}, f32[19,128]{1,0:T(8,128)S(1)}, f32[1,128]{1,0:T(1,128)S(1)}, f32[128,128]{1,...) custom-call(f32[304,128]{1,0:T(8,128)S(1)} %bitcast.9, ...), custom_call_target="tpu_custom_call" | custom-call | tf_op jit(solution)/shard_map/pallas_call | solution.py:537
  39.9 0.7 %copy.20 = f32[128,19]{0,1:T(8,128)} copy(f32[128,19]{1,0:T(8,128)S(1)} %get-tuple-element.30) | data formatting | bytes 19456
  40.5 0.7 %copy.28 = f32[19,2,8,128]{3,2,1,0:T(8,128)} copy(f32[19,2,8,128]{3,2,1,0:T(8,128)S(1)} %bitcast.11) | data formatting | bytes 311296
  41.2 0.6 %copy.29 = f32[2,8,128]{2,1,0:T(8,128)} copy(f32[2,8,128]{2,1,0:T(8,128)S(1)} %get-tuple-element.41) | data formatting | bytes 16384
  41.8 0.6 %copy.30 = f32[19,128]{1,0:T(8,128)} copy(f32[19,128]{1,0:T(8,128)S(1)} %get-tuple-element.42) | data formatting | bytes 19456
  42.4 0.5 %copy.31 = f32[128]{0:T(128)} copy(f32[128]{0:T(128)S(1)} %bitcast.17) | data formatting | bytes 1024
  42.9 0.6 %copy.32 = f32[128,128]{1,0:T(8,128)} copy(f32[128,128]{1,0:T(8,128)S(1)} %get-tuple-element.44) | data formatting | bytes 131072
  43.5 0.5 %copy.33 = f32[128]{0:T(128)} copy(f32[128]{0:T(128)S(1)} %bitcast.16) | data formatting | bytes 1024
  44.1 0.5 %copy.34 = f32[19]{0:T(128)} copy(f32[19]{0:T(128)S(1)} %bitcast.15) | data formatting | bytes 152
Async XLA Ops:
  0.6 0.9 %copy-start.2 = (f32[128,128]{1,0:T(8,128)S(1)}, f32[128,128]{1,0:T(8,128)}, u32[]{:S(2)}) copy-start(f32[128,128]{1,0:T(8,128)} %w2.1) | copy-start | bytes 196612
  0.6 0.9 %copy-start.3 = (f32[19,128]{1,0:T(8,128)S(1)}, f32[19,128]{1,0:T(8,128)}, u32[]{:S(2)}) copy-start(f32[19,128]{1,0:T(8,128)} %w1.1) | copy-start | bytes 29188
  0.7 0.9 %copy-start.4 = (f32[2,8,128]{2,1,0:T(8,128)S(1)}, f32[2,8,128]{2,1,0:T(8,128)}, u32[]{:S(2)}) copy-start(f32[2,8,128]{2,1,0:T(8,128)} %t0.1) | copy-start | bytes 24580
  0.7 0.9 %copy-start.7 = (f32[128]{0:T(128)S(1)}, f32[128]{0:T(128)}, u32[]{:S(2)}) copy-start(f32[128]{0:T(128)} %param.15) | copy-start | bytes 1540
  0.7 0.9 %copy-start.8 = (f32[128]{0:T(128)S(1)}, f32[128]{0:T(128)}, u32[]{:S(2)}) copy-start(f32[128]{0:T(128)} %param.17) | copy-start | bytes 1540
  1.6 0.9 %copy-start = (f32[19,2,8,128]{3,2,1,0:T(8,128)S(1)}, f32[19,2,8,128]{3,2,1,0:T(8,128)}, u32[]{:S(2)}) copy-start(f32[19,2,8,128]{3,2,1,0:T(8,128)} %param.11) | copy-start | bytes 466948
  2.5 0.9 %copy-start.1 = (f32[19,2,8,128]{3,2,1,0:T(8,128)S(1)}, f32[19,2,8,128]{3,2,1,0:T(8,128)}, u32[]{:S(2)}) copy-start(f32[19,2,8,128]{3,2,1,0:T(8,128)} %param.20) | copy-start | bytes 466948
  3.4 0.7 %copy-start.5 = (s32[2,8,128]{2,1,0:T(8,128)S(1)}, s32[2,8,128]{2,1,0:T(8,128)}, u32[]{:S(2)}) copy-start(s32[2,8,128]{2,1,0:T(8,128)} %site.1) | copy-start | bytes 24580
  4.1 0.7 %copy-start.6 = (f32[2,8,128]{2,1,0:T(8,128)S(1)}, f32[2,8,128]{2,1,0:T(8,128)}, u32[]{:S(2)}) copy-start(f32[2,8,128]{2,1,0:T(8,128)} %tadj2.1) | copy-start | bytes 24580
  4.8 0.7 %copy-start.9 = (f32[19]{0:T(128)S(1)}, f32[19]{0:T(128)}, u32[]{:S(2)}) copy-start(f32[19]{0:T(128)} %param.19) | copy-start | bytes 232

commit v2 on v1

--- a/solution.py
+++ b/solution.py
@@ -75,10 +75,12 @@
 
 def kernel(
     sizes,
-    f0, t0, site, w1, b1, w2, b2, w3, b3, adj2, tadj2,
-    adj_out, tadj_out, gw1, gb1, gw2, gb2, gw3, gb3,
+    f0_in, t0_in, site_in, w1_in, b1_in, w2_in, b2_in, w3_in, b3_in, adj2_in, tadj2_in,
+    adj_to, tadj_to, gw1_to, gb1_to, gw2_to, gb2_to, gw3_to, gb3_to,
+    adj_out, tadj_out, gw1, gb1, gw2, gb2, gw3, gb3, stored,
+    f0, t0, site, w1, b1, w2, b2, w3, b3, adj2, tadj2, loaded,
     post, f1, t1, adj1, tadj1, net, pcg, pcgf,
-    ft, pt, h1, h2, h1c, h2c, d1c, d2c,
+    ft, pt, back, h1, h2, h1c, h2c, d1c, d2c,
     square, m1, m2, m3, r1, r2, r3, col,
     sx, sy, sc, rx, ry, rc, send, recv,
     grads, parts_y, parts_x, total, gsend, grecv,
@@ -89,14 +91,33 @@
     hid = w2.shape[0]
     chunk = min(4, cols)
     gx, gy = lax.axis_index("gx"), lax.axis_index("gy")
+    arguments = [
+        (w1_in, w1), (b1_in, b1), (w2_in, w2), (b2_in, b2), (w3_in, w3), (b3_in, b3),
+        (f0_in, f0), (t0_in, t0), (site_in, site), (adj2_in, adj2), (tadj2_in, tadj2),
+    ]
+    loads = [
+        pltpu.make_async_copy(src, dst, loaded.at[k]) for k, (src, dst) in enumerate(arguments)
+    ]
+    for c in loads:
+        c.start()
 
     def device(dx, dy):
         return (lax.rem(gx + dx + ngx, ngx), lax.rem(gy + dy + ngy, ngy))
 
     barrier = pltpu.get_barrier_semaphore()
-    partners = [(d, 0) for d in range(1, ngx)] + [(0, d) for d in range(1, ngy)] + CORNERS
-    for dx, dy in partners:
-        pl.semaphore_signal(barrier, inc=1, device_id=device(dx, dy), device_id_type=MESH)
+    duo = 2 if ngx % 2 == 0 else 1
+    spot = lax.rem(gx, duo)
+
+    def near(dx, dy):
+        return (gx - spot + lax.rem(spot + dx, duo), lax.rem(gy + dy, ngy))
+
+    inner = [(dx, dy) for dx in range(duo) for dy in range(ngy)][1:]
+    outer = ngx // duo
+    partners = [device(dx, dy) for dx, dy in [(1, 0), (-1, 0), (0, 1), (0, -1)] + CORNERS]
+    partners += [near(dx, dy) for dx, dy in inner]
+    partners += [device(duo * d, 0) for d in range(1, outer)]
+    for partner in partners:
+        pl.semaphore_signal(barrier, inc=1, device_id=partner, device_id_type=MESH)
 
     def rows(i, x):
         return pl.ds((i * nx + x) * ny, ny)
@@ -107,7 +128,14 @@
     depth = lax.broadcasted_iota(jnp.int32, (ny, nz), 1)
     height = lax.broadcasted_iota(jnp.int32, (ny, nz), 0)
 
+    for s in range(2):
+        ft[s] = jnp.zeros((ROWS, sites), F32)
+        ft[s, Q : Q + 1, :] = jnp.ones((1, sites), F32)
+    pt[...] = jnp.zeros_like(pt)
+    grads[...] = jnp.zeros_like(grads)
     square[...] = jnp.zeros_like(square)
+    for c in loads[:6]:
+        c.wait()
     square[0:Q, :] = w1[...]
     square[Q : Q + 1, :] = b1[...]
     w1_rows = square[...]
@@ -124,23 +152,18 @@
             axis=0,
         )
     square[...] = jnp.zeros_like(square)
-    square[:, 0:Q] = w3[...]
-    w3_cols = square[...]
-    a, b = halves(jnp.transpose(w3_cols)[:ROWS])
+    square[0:Q, :] = w3[...]
+    w3_rows = square[...]
+    a, b = halves(w3_rows[:ROWS])
     m3[...] = jnp.concatenate(
         [jnp.concatenate([a, a], axis=1), jnp.concatenate([b, jnp.zeros_like(b)], axis=1)], axis=0
     )
-    a, b = halves(w3_cols[:, :ROWS])
+    a, b = halves(jnp.transpose(w3_rows)[:, :ROWS])
     r3[...] = jnp.concatenate([a, a, b], axis=1)
     square[...] = jnp.zeros_like(square)
     square[0:1, :] = b2[...]
     square[1:2, 0:Q] = b3[...]
     col[...] = jnp.transpose(square[...])
-
-    for s in range(2):
-        ft[s] = jnp.zeros((ROWS, sites), F32)
-        ft[s, Q : Q + 1, :] = jnp.ones((1, sites), F32)
-    pt[...] = jnp.zeros_like(pt)
 
     def to_rows(source, target):
         for c in range(cols):
@@ -167,45 +190,46 @@
         h2c[s, :, at] = pair
         return pair
 
-    def network_back(s, first, at):
-        a, b = halves(pt[s, :, at])
-        back = dot(r3[...], jnp.concatenate([a, b, a], axis=0), NN)
+    def network_back(s, at):
         two = h2[s, :, at]
-        pair = jnp.concatenate(halves(back * (1.0 - two * two)), axis=0)
+        pair = jnp.concatenate(halves(back[:, at] * (1.0 - two * two)), axis=0)
         d2c[s, :, at] = pair
         both = dot(r2[...], pair, NN)
         one = h1[s, :, at]
         pair = jnp.concatenate(halves((both[:hid] + both[hid:]) * (1.0 - one * one)), axis=0)
         d1c[s, :, at] = pair
-        both = dot(r1[...], pair, NN)
-        to_planes(both[:ROWS] + both[ROWS:], first, net)
+
+    def network_in(s):
+        for first, at in chunks():
+            both = dot(r1[...], d1c[s, :, at], NN)
+            to_planes(both[:ROWS] + both[ROWS:], first, net)
 
     def folded(product, n, m):
         return product[:n, :m] + product[:n, m : 2 * m] + product[n : 2 * n, :m]
 
-    at1, at2 = 0, ROWS
+    at2 = 24
     at3 = at2 + hid
-    at4 = at3 + 8
-    at5 = at4 + ROWS
+    at4 = at3 + Q
 
     def weight_grads(s):
+        ones = jnp.ones((16, sites), BF16)
         pairs = dot(jnp.concatenate(halves(ft[s]), axis=0), d1c[s], NT)
-        first = folded(pairs, ROWS, hid)
-        ones = jnp.ones((16, sites), BF16)
+        first = folded(pairs, ROWS, hid)[: Q + 1]
         pairs = dot(jnp.concatenate([h1c[s], ones], axis=0), d2c[s], NT)
         second = folded(pairs, hid, hid)
-        second_bias = pairs[2 * hid : 2 * hid + 8, :hid] + pairs[2 * hid : 2 * hid + 8, hid:]
-        pairs = dot(jnp.concatenate(halves(pt[s]), axis=0), h2c[s], NT)
-        third = folded(pairs, ROWS, hid)
-        third_bias = jnp.broadcast_to(jnp.sum(pt[s], axis=1, keepdims=True), (ROWS, LANES))
+        second_bias = (pairs[2 * hid :, :hid] + pairs[2 * hid :, hid:])[0:1]
+        split = jnp.concatenate(halves(pt[s]), axis=0)
+        third = folded(dot(split, h2c[s], NT), ROWS, hid)[:Q]
+        pairs = dot(ones, split, NT)
+        third_bias = (pairs[:, :ROWS] + pairs[:, ROWS:])[0:1]
         for start, value in (
-            (at1, first), (at2, second), (at3, second_bias), (at4, third), (at5, third_bias)
+            (0, first), (at2, second), (at3, third), (at4, second_bias), (at4 + 1, third_bias)
         ):
-            where = pl.ds(start, value.shape[0])
+            n, m = value.shape
             if s == 1:
-                grads[where, :] = value
+                grads[start : start + n, :m] = value
             else:
-                grads[where, :] = (grads[where, :] + value) * factor
+                grads[start : start + n, :m] = (grads[start : start + n, :m] + value) * factor
 
     started = []
 
@@ -334,11 +358,19 @@
     def flux(fields, tadj, x, a, s):
         return (CONDUCTIVITY - 0.5 * s * motion(fields, x)[a]) * liquid(tadj, x)
 
+    loads[6].wait()
     to_rows(f0, ft.at[0])
+    halfway = (cols // chunk) // 2 * chunk
     for first, at in chunks():
+        if first == halfway:
+            loads[9].wait()
+            pl.semaphore_wait(barrier, len(partners))
+            copies_0 = begin(1, adj2, -1, [], True)
         pair = hidden(0, at)
         both = dot(m3[...], pair, NN)
         to_planes(both[:ROWS] + both[ROWS:] + col[:ROWS, 1:2], first, net)
+    for c in loads[7:9] + loads[10:]:
+        c.wait()
     for x in range(nx):
         open_cell = fluid(x)
         for i in range(Q):
@@ -346,10 +378,28 @@
             if BUOYANCY[i] != 0.0:
                 value = value + BUOYANCY[i] * t0[x]
             post[rows(i, x), :] = jnp.where(open_cell, value, f0[rows(OPPOSITE[i], x), :])
-    pl.semaphore_wait(barrier, len(partners))
     copies_a = begin(0, post, 1, [lambda a, s, x: t0[x]], True)
-    copies_0 = begin(1, adj2, -1, [], True)
+
+    def incoming(s, adjoint, e_adj):
+        lifts = [jnp.zeros((ny, nz), F32) for _ in range(nx)]
+
+        def keep(i, x, plane):
+            pcg[rows(i, x), :] = plane
+            value = jnp.where(fluid(x), plane, 0.0)
+            pcgf[rows(i, x), :] = value
+            if BUOYANCY[i] != 0.0:
+                lifts[x] = lifts[x] + BUOYANCY[i] * value
+
+        stream(adjoint, e_adj, -1, keep)
+        to_rows(pcgf, pt.at[s])
+        for first, at in chunks():
+            a, b = halves(pt[s, :, at])
+            back[:, at] = dot(r3[...], jnp.concatenate([a, b, a], axis=0), NN)
+        return lifts
+
     speeds0 = [motion(f0, x) for x in range(nx)]
+    arrive(copies_0)
+    lifts = incoming(1, adj2, 1)
     arrive(copies_a)
 
     def keep_f1(i, x, plane):
@@ -372,23 +422,10 @@
     to_rows(f1, ft.at[1])
     for first, at in chunks():
         hidden(1, at)
-
-    def step_back(s, fields, field, adjoint, tadj, e_adj, e_heat, heat_slot, e_flux, flux_slot,
-                  waits, new_adj, new_tadj):
-        lifts = [jnp.zeros((ny, nz), F32) for _ in range(nx)]
-
-        def keep(i, x, plane):
-            pcg[rows(i, x), :] = plane
-            value = jnp.where(fluid(x), plane, 0.0)
-            pcgf[rows(i, x), :] = value
-            if BUOYANCY[i] != 0.0:
-                lifts[x] = lifts[x] + BUOYANCY[i] * value
-
-        stream(adjoint, e_adj, -1, keep)
-        to_rows(pcgf, pt.at[s])
-        for first, at in chunks():
-            network_back(s, first, at)
-        arrive(waits)
+        network_back(1, at)
+
+    def assemble(fields, field, tadj, e_heat, heat_slot, e_flux, flux_slot, lifts, new_adj,
+                 new_tadj):
         for x in range(nx):
             wet = liquid(tadj, x)
             speed = motion(fields, x)
@@ -423,66 +460,96 @@
                         value = value - pulls[a]
                 new_adj[rows(i, x), :] = value
 
-    arrive(copies_0)
-    step_back(1, f1, t1, adj2, tadj2, 1, 2, 0, 2, 1, copies_b, adj1, tadj1)
+    network_in(1)
+    arrive(copies_b)
+    assemble(f1, t1, tadj2, 2, 0, 2, 1, lifts, adj1, tadj1)
     copies_c = begin(3, adj1, -1, [lambda a, s, x: flux(f0, tadj1, x, a, s)], True)
     weight_grads(1)
     arrive(copies_c)
-    step_back(0, f0, t0, adj1, tadj1, 3, 0, 5, 3, 5, [], adj_out, tadj_out)
+    lifts = incoming(0, adj1, 3)
+    for first, at in chunks():
+        network_back(0, at)
+    results = [
+        (adj_out, adj_to), (tadj_out, tadj_to), (gw1, gw1_to), (gb1, gb1_to),
+        (gw2, gw2_to), (gb2, gb2_to), (gw3, gw3_to), (gb3, gb3_to),
+    ]
+    stores = [
+        pltpu.make_async_copy(src, dst, stored.at[k]) for k, (src, dst) in enumerate(results)
+    ]
     weight_grads(0)
 
-    part = grads.shape[0] // ngy
-    if at5 + ROWS < grads.shape[0]:
-        grads[at5 + ROWS :, :] = jnp.zeros((grads.shape[0] - at5 - ROWS, LANES), F32)
-
-    def block(index):
+    part = grads.shape[0] // (duo * ngy)
+
+    def block(where):
+        index = (where[0] - (gx - spot)) * ngy + where[1]
         return pl.ds(pl.multiple_of(index * part, 8), part)
 
-    def share(src, dst, n, dx, dy):
+    def share(src, dst, n, target):
         c = pltpu.make_async_remote_copy(
             src_ref=src, dst_ref=dst, send_sem=gsend.at[n], recv_sem=grecv.at[n],
-            device_id=device(dx, dy), device_id_type=MESH,
+            device_id=target, device_id_type=MESH,
         )
         c.start()
         started.append(c)
         return c
 
+    mine = block((gx, gy))
     copies = []
-    for d in range(1, ngy):
-        copies.append(
-            share(grads.at[block(lax.rem(gy + d, ngy))], parts_y.at[d - 1], d - 1, 0, d)
-        )
-    value = grads[block(gy), :]
-    arrive(copies)
-    for d in range(1, ngy):
-        value = value + parts_y[d - 1]
+    for n, (dx, dy) in enumerate(inner):
+        copies.append(share(grads.at[block(near(dx, dy))], parts_y.at[n], n, near(dx, dy)))
+    network_in(0)
+    assemble(f0, t0, tadj1, 0, 5, 3, 5, lifts, adj_out, tadj_out)
+    for c in stores[:2]:
+        c.start()
+    value = grads[mine, :]
+    for n, c in enumerate(copies):
+        c.wait_recv()
+        value = value + parts_y[n]
     parts_x[0] = value
     copies = []
-    for d in range(1, ngx):
-        copies.append(share(parts_x.at[0], parts_x.at[d], ngy - 1 + d - 1, d, 0))
+    for d in range(1, outer):
+        copies.append(
+            share(parts_x.at[0], parts_x.at[d], len(inner) + d - 1, device(duo * d, 0))
+        )
     arrive(copies)
     value = None
-    for k in range(ngx):
-        term = parts_x[lax.rem(gx - k + ngx, ngx)]
+    for k in range(outer):
+        term = parts_x[lax.rem((gx - spot) // duo - k + outer, outer)]
         value = term if value is None else value + term
-    total[block(gy), :] = value
+    total[mine, :] = value
     copies = []
-    for d in range(1, ngy):
+    for n, (dx, dy) in enumerate(inner):
         copies.append(
-            share(total.at[block(gy)], total.at[block(gy)], ngy + ngx - 2 + d - 1, 0, d)
+            share(total.at[mine], total.at[mine], len(inner) + outer - 1 + n, near(dx, dy))
         )
     arrive(copies)
-    gw1[...] = total[at1 : at1 + Q, :]
-    gb1[...] = total[at1 + Q : at1 + Q + 1, :]
+    gw1[...] = total[0:Q, :]
+    gb1[...] = total[Q : Q + 1, :]
     gw2[...] = total[at2 : at2 + hid, :]
-    gb2[...] = total[at3 : at3 + 1, :]
-    square[...] = jnp.zeros_like(square)
-    square[0:ROWS, :] = total[at4 : at4 + ROWS, :]
-    gw3[...] = jnp.transpose(square[...])[:, 0:Q]
-    square[0:ROWS, :] = total[at5 : at5 + ROWS, :]
-    gb3[...] = jnp.transpose(square[...])[0:1, 0:Q]
+    gw3[...] = total[at3 : at3 + Q, :]
+    gb2[...] = total[at4 : at4 + 1, :]
+    gb3[...] = total[at4 + 1 : at4 + 2, 0:Q]
+    for c in stores[2:]:
+        c.start()
     for c in started:
         c.wait_send()
+    for c in stores:
+        c.wait()
+
+
+def hand_out(*refs):
+    load, store = refs[-2:]
+    n = (len(refs) - 2) // 3
+    ins, outs, held = refs[:n], refs[n : 2 * n], refs[2 * n : 3 * n]
+    loads = [pltpu.make_async_copy(ins[k], held[k], load.at[k]) for k in range(n)]
+    stores = [pltpu.make_async_copy(held[k], outs[k], store.at[k]) for k in range(n)]
+    for c in loads:
+        c.start()
+    for k in range(n):
+        loads[k].wait()
+        stores[k].start()
+    for c in stores:
+        c.wait()
 
 
 def per_device(ngx, ngy, f0, t0, site, w1, b1, w2, b2, w3, b3, adj2, tadj2):
@@ -491,18 +558,29 @@
     sites = nx * ny * nz
     flat = (q * nx * ny, nz)
     factor = 1.0 / math.sqrt(nx * ngx * ny * ngy * nz)
-    needed = 3 * ROWS + hid + 8
-    unit = 8 * ngy
+    group = (2 if ngx % 2 == 0 else 1) * ngy
+    outer = ngx * ngy // group
+    needed = 24 + hid + 24
+    unit = 8 * group
     length = -(-needed // unit) * unit
     side = -(-(SLOTS * nx) // 8) * 8
     plane = pltpu.VMEM((nx, ny, nz), F32)
     wide = pltpu.VMEM(flat, F32)
     dma = pltpu.SemaphoreType.DMA
-    gcount = 2 * (ngy - 1) + ngx - 1
+    gcount = 2 * (group - 1) + outer - 1
     scratch = [
+        wide, plane, pltpu.VMEM(w1.shape, F32), pltpu.VMEM((1, hid), F32),
+        pltpu.VMEM(w2.shape, F32), pltpu.VMEM((1, hid), F32),
+        pltpu.VMEM((q, hid), F32), pltpu.VMEM((1, q), F32), dma((8,)),
+        wide, plane, pltpu.VMEM((nx, ny, nz), jnp.int32),
+        pltpu.VMEM(w1.shape, F32), pltpu.VMEM((1, hid), F32),
+        pltpu.VMEM(w2.shape, F32), pltpu.VMEM((1, hid), F32),
+        pltpu.VMEM((q, hid), F32), pltpu.VMEM((1, q), F32),
+        wide, plane, dma((11,)),
         wide, wide, plane, wide, plane, wide, wide, wide,
         pltpu.VMEM((2, ROWS, sites), F32),
         pltpu.VMEM((2, ROWS, sites), F32),
+        pltpu.VMEM((hid, sites), F32),
         pltpu.VMEM((2, hid, sites), F32),
         pltpu.VMEM((2, hid, sites), F32),
         pltpu.VMEM((2, 2 * hid, sites), BF16),
@@ -526,35 +604,44 @@
         dma((4, 8)),
         dma((4, 8)),
         pltpu.VMEM((length, LANES), F32),
-        pltpu.VMEM((ngy - 1, length // ngy, LANES), F32),
-        pltpu.VMEM((ngx, length // ngy, LANES), F32),
+        pltpu.VMEM((group - 1, length // group, LANES), F32),
+        pltpu.VMEM((outer, length // group, LANES), F32),
         pltpu.VMEM((length, LANES), F32),
         dma((gcount,)),
         dma((gcount,)),
     ]
     shape = jax.ShapeDtypeStruct
-    vmem = pl.BlockSpec(memory_space=pltpu.VMEM)
+    anywhere = pl.BlockSpec(memory_space=pltpu.HBM)
+    shapes = [
+        shape(flat, F32), shape((nx, ny, nz), F32),
+        shape(w1.shape, F32), shape((1, hid), F32),
+        shape(w2.shape, F32), shape((1, hid), F32),
+        shape((q, hid), F32), shape((1, q), F32),
+    ]
     outs = pl.pallas_call(
         functools.partial(kernel, (nx, ny, nz, ngx, ngy, factor)),
-        out_shape=[
-            shape(flat, F32), shape((nx, ny, nz), F32),
-            shape(w1.shape, F32), shape((1, hid), F32),
-            shape(w2.shape, F32), shape((1, hid), F32),
-            shape(w3.shape, F32), shape((1, q), F32),
-        ],
-        in_specs=[vmem] * 11,
-        out_specs=[vmem] * 8,
+        out_shape=shapes,
+        in_specs=[anywhere] * 11,
+        out_specs=[anywhere] * 8,
         scratch_shapes=scratch,
         compiler_params=pltpu.CompilerParams(
-            collective_id=0, has_side_effects=True, vmem_limit_bytes=48 * 1024 * 1024
+            collective_id=0, has_side_effects=True, vmem_limit_bytes=64 * 1024 * 1024
         ),
     )(
         f0.reshape(flat), t0, site, w1, b1.reshape(1, hid), w2, b2.reshape(1, hid),
-        w3, b3.reshape(1, q), adj2.reshape(flat), tadj2,
+        w3.T, b3.reshape(1, q), adj2.reshape(flat), tadj2,
     )
+    outs = pl.pallas_call(
+        hand_out,
+        out_shape=shapes,
+        in_specs=[anywhere] * 8,
+        out_specs=[anywhere] * 8,
+        scratch_shapes=[pltpu.VMEM(s.shape, s.dtype) for s in shapes] + [dma((8,)), dma((8,))],
+        compiler_params=pltpu.CompilerParams(vmem_limit_bytes=64 * 1024 * 1024),
+    )(*outs)
     return (
         outs[0].reshape(f0.shape), outs[1], outs[2], outs[3].reshape(hid),
-        outs[4], outs[5].reshape(hid), outs[6], outs[7].reshape(q),
+        outs[4], outs[5].reshape(hid), outs[6].T, outs[7].reshape(q),
     )
 
 

time: 44.9 us -> 37 us (0.82)
  local copies, waits for them, and re-layouts: 9.44 us -> 0 us
  Pallas kernels: 34.4 us -> 36.2 us
    unnamed x29 -> x0, local copies, waits for them, and re-layouts: 9.44 us -> none
    pallas_call x0 -> x1, Pallas kernels: none -> 1.75 us  [per_device(): pl.pallas_call(hand_out, out_shape=shapes, in_specs=[anywhere] * 8, out_s...]
where the time goes in v2:
time: 37 us; the launch traced here: 36.8 us
  Pallas kernels  36.2 us (98%)
  between operations  0.65 us (2%)
    pallas_call x1, Pallas kernels, per_device(): pl.pallas_call(functools.partial(kernel, (nx, ny, nz, ngx, ngy, factor)),...  34.4 us
    pallas_call x1, Pallas kernels, per_device(): pl.pallas_call(hand_out, out_shape=shapes, in_specs=[anywhere] * 8, out_s...  1.75 us

profile of v2, /device:TPU:0, one launch (start us, length us, event | category | flops | bytes accessed | tf_op | source)
XLA Modules:
  0.0 36.8 jit_solution(11822507093208498936)
XLA Ops:
  0.6 34.4 %shard_map.170 = (f32[304,128]{1,0:T(8,128)}, f32[2,8,128]{2,1,0:T(8,128)}, f32[19,128]{1,0:T(8,128)}, f32[1,128]{1,0:T(1,128)}, f32[128,128]{1,0:T(8,128)}, /*i...) custom-call(f32[304,128]{1,0:T(8,128)} %bitcast.11, f32[2,8,128]{2,1,0:T(8,128)} %t0_in.1, ...), custom_call_target="tpu_custom_call" | custom-call | tf_op jit(solution)/shard_map/pallas_call | solution.py:621
  35.1 1.8 %shard_map.171 = (f32[304,128]{1,0:T(8,128)}, f32[2,8,128]{2,1,0:T(8,128)}, f32[19,128]{1,0:T(8,128)}, f32[1,128]{1,0:T(1,128)}, f32[128,128]{1,0:T(8,128)}, /*i...) custom-call(f32[304,128]{1,0:T(8,128)} %get-tuple-element.24.refs_0_, f32[2,8,128]{2,1,0:T(8,128)} %get-tuple-element.25.refs_1_, ...), custom_call_target="tpu_custom_call" | custom-call | tf_op jit(solution)/shard_map/pallas_call | solution.py:634

commit v3 on v2

--- a/solution.py
+++ b/solution.py
@@ -89,7 +89,6 @@
     cols = nx * ny
     sites = cols * nz
     hid = w2.shape[0]
-    chunk = min(4, cols)
     gx, gy = lax.axis_index("gx"), lax.axis_index("gy")
     arguments = [
         (w1_in, w1), (b1_in, b1), (w2_in, w2), (b2_in, b2), (w3_in, w3), (b3_in, b3),
@@ -131,6 +130,7 @@
     for s in range(2):
         ft[s] = jnp.zeros((ROWS, sites), F32)
         ft[s, Q : Q + 1, :] = jnp.ones((1, sites), F32)
+        h1c[s, 2 * hid :, :] = jnp.ones((16, sites), BF16)
     pt[...] = jnp.zeros_like(pt)
     grads[...] = jnp.zeros_like(grads)
     square[...] = jnp.zeros_like(square)
@@ -170,10 +170,10 @@
             target[0:Q, c * nz : (c + 1) * nz] = source[pl.ds(c, Q, stride=cols), :]
 
     def to_planes(values, first, target):
-        for c in range(chunk):
+        for c in range(values.shape[1] // nz):
             target[pl.ds(first + c, Q, stride=cols), :] = values[0:Q, c * nz : (c + 1) * nz]
 
-    def chunks():
+    def chunks(chunk=cols):
         for first in range(0, cols, chunk):
             yield first, pl.ds(first * nz, chunk * nz)
 
@@ -182,7 +182,7 @@
         one = jnp.tanh(dot(m1[...], jnp.concatenate([a, b, a], axis=0), NN))
         h1[s, :, at] = one
         pair = jnp.concatenate(halves(one), axis=0)
-        h1c[s, :, at] = pair
+        h1c[s, 0 : 2 * hid, at] = pair
         both = dot(m2[...], pair, NN)
         two = jnp.tanh(both[:hid] + both[hid:] + col[:, 0:1])
         h2[s, :, at] = two
@@ -212,10 +212,10 @@
     at4 = at3 + Q
 
     def weight_grads(s):
-        ones = jnp.ones((16, sites), BF16)
+        ones = h1c[s, 2 * hid :, :]
         pairs = dot(jnp.concatenate(halves(ft[s]), axis=0), d1c[s], NT)
         first = folded(pairs, ROWS, hid)[: Q + 1]
-        pairs = dot(jnp.concatenate([h1c[s], ones], axis=0), d2c[s], NT)
+        pairs = dot(h1c[s], d2c[s], NT)
         second = folded(pairs, hid, hid)
         second_bias = (pairs[2 * hid :, :hid] + pairs[2 * hid :, hid:])[0:1]
         split = jnp.concatenate(halves(pt[s]), axis=0)
@@ -355,14 +355,13 @@
     def liquid(tadj, x):
         return jnp.where(fluid(x), tadj[x], 0.0)
 
-    def flux(fields, tadj, x, a, s):
-        return (CONDUCTIVITY - 0.5 * s * motion(fields, x)[a]) * liquid(tadj, x)
+    def flux(speeds, tadj, x, a, s):
+        return (CONDUCTIVITY - 0.5 * s * speeds[x][a]) * liquid(tadj, x)
 
     loads[6].wait()
     to_rows(f0, ft.at[0])
-    halfway = (cols // chunk) // 2 * chunk
-    for first, at in chunks():
-        if first == halfway:
+    for first, at in chunks(ny):
+        if first == nx // 2 * ny:
             loads[9].wait()
             pl.semaphore_wait(barrier, len(partners))
             copies_0 = begin(1, adj2, -1, [], True)
@@ -414,9 +413,10 @@
                     t0, 0, 5, x, a, s
                 )
         t1[x] = jnp.where(fluid(x), value, jnp.where(site[x] == 1, t0[x], HEATER))
+    speeds1 = [motion(f1, x) for x in range(nx)]
     copies_b = begin(
         2, None, 1,
-        [lambda a, s, x: t1[x], lambda a, s, x: flux(f1, tadj2, x, a, s)], False,
+        [lambda a, s, x: t1[x], lambda a, s, x: flux(speeds1, tadj2, x, a, s)], False,
     )
 
     to_rows(f1, ft.at[1])
@@ -424,17 +424,17 @@
         hidden(1, at)
         network_back(1, at)
 
-    def assemble(fields, field, tadj, e_heat, heat_slot, e_flux, flux_slot, lifts, new_adj,
+    def assemble(speeds, field, tadj, e_heat, heat_slot, e_flux, flux_slot, lifts, new_adj,
                  new_tadj):
         for x in range(nx):
             wet = liquid(tadj, x)
-            speed = motion(fields, x)
+            speed = speeds[x]
             value = (1.0 - 6.0 * CONDUCTIVITY) * wet + jnp.where(site[x] == 1, tadj[x], 0.0)
             for a in range(3):
                 for sign in SIGNS:
                     if a == 0:
                         value = value + moved_x(
-                            lambda k: flux(fields, tadj, k, 0, sign), e_flux, flux_slot, x, sign
+                            lambda k: flux(speeds, tadj, k, 0, sign), e_flux, flux_slot, x, sign
                         )
                         continue
                     here = (CONDUCTIVITY - 0.5 * sign * speed[a]) * wet
@@ -462,8 +462,8 @@
 
     network_in(1)
     arrive(copies_b)
-    assemble(f1, t1, tadj2, 2, 0, 2, 1, lifts, adj1, tadj1)
-    copies_c = begin(3, adj1, -1, [lambda a, s, x: flux(f0, tadj1, x, a, s)], True)
+    assemble(speeds1, t1, tadj2, 2, 0, 2, 1, lifts, adj1, tadj1)
+    copies_c = begin(3, adj1, -1, [lambda a, s, x: flux(speeds0, tadj1, x, a, s)], True)
     weight_grads(1)
     arrive(copies_c)
     lifts = incoming(0, adj1, 3)
@@ -498,7 +498,7 @@
     for n, (dx, dy) in enumerate(inner):
         copies.append(share(grads.at[block(near(dx, dy))], parts_y.at[n], n, near(dx, dy)))
     network_in(0)
-    assemble(f0, t0, tadj1, 0, 5, 3, 5, lifts, adj_out, tadj_out)
+    assemble(speeds0, t0, tadj1, 0, 5, 3, 5, lifts, adj_out, tadj_out)
     for c in stores[:2]:
         c.start()
     value = grads[mine, :]
@@ -583,7 +583,7 @@
         pltpu.VMEM((hid, sites), F32),
         pltpu.VMEM((2, hid, sites), F32),
         pltpu.VMEM((2, hid, sites), F32),
-        pltpu.VMEM((2, 2 * hid, sites), BF16),
+        pltpu.VMEM((2, 2 * hid + 16, sites), BF16),
         pltpu.VMEM((2, 2 * hid, sites), BF16),
         pltpu.VMEM((2, 2 * hid, sites), BF16),
         pltpu.VMEM((2, 2 * hid, sites), BF16),

time: 37 us -> 36.7 us (level)
  Pallas kernels: 36.2 us -> 35.8 us
    pallas_call x1, Pallas kernels: 34.4 us -> 34 us  [per_device(): pl.pallas_call(functools.partial(kernel, (nx, ny, nz, ngx, ngy, factor)),...]
where the time goes in v3:
time: 36.7 us; the launch traced here: 36.4 us
  Pallas kernels  35.8 us (98%)
  between operations  0.65 us (2%)
    pallas_call x1, Pallas kernels, per_device(): pl.pallas_call(functools.partial(kernel, (nx, ny, nz, ngx, ngy, factor)),...  34 us
    pallas_call x1, Pallas kernels, per_device(): pl.pallas_call(hand_out, out_shape=shapes, in_specs=[anywhere] * 8, out_s...  1.75 us

profile of v3, /device:TPU:0, one launch (start us, length us, event | category | flops | bytes accessed | tf_op | source)
XLA Modules:
  0.0 36.4 jit_solution(10604873323756117232)
XLA Ops:
  0.6 34.0 %shard_map.170 = (f32[304,128]{1,0:T(8,128)}, f32[2,8,128]{2,1,0:T(8,128)}, f32[19,128]{1,0:T(8,128)}, f32[1,128]{1,0:T(1,128)}, f32[128,128]{1,0:T(8,128)}, /*i...) custom-call(f32[304,128]{1,0:T(8,128)} %bitcast.11, f32[2,8,128]{2,1,0:T(8,128)} %t0_in.1, ...), custom_call_target="tpu_custom_call" | custom-call | tf_op jit(solution)/shard_map/pallas_call | solution.py:621
  34.7 1.8 %shard_map.171 = (f32[304,128]{1,0:T(8,128)}, f32[2,8,128]{2,1,0:T(8,128)}, f32[19,128]{1,0:T(8,128)}, f32[1,128]{1,0:T(1,128)}, f32[128,128]{1,0:T(8,128)}, /*i...) custom-call(f32[304,128]{1,0:T(8,128)} %get-tuple-element.24.refs_0_, f32[2,8,128]{2,1,0:T(8,128)} %get-tuple-element.25.refs_1_, ...), custom_call_target="tpu_custom_call" | custom-call | tf_op jit(solution)/shard_map/pallas_call | solution.py:634
